TPU v7x, 128 devices: a whole 4x4x4 slice. The times are simulated.
128 devices in a mesh: ctx: 8 (over z_hi, x), fsdp: 16 (over y, z_lo, core).
Axes of the slice: x: 4, y: 4, z: 4 (z_hi: 2, z_lo: 2; z = z_hi * 2 + z_lo), core: 2. Of those that a mesh axis runs over, the one named last changes fastest.
Arguments:
- layer_input: bfloat16 [16, 1024, 2048], P('fsdp', 'ctx'), may hold values from -6 to 6
- cotangent: bfloat16 [16, 1024, 2048], P('fsdp', 'ctx'), may hold values from -6 to 6
- query_weight: bfloat16 [2048, 2048], P('fsdp'), may hold values from -0.125 to 0.125
- key_weight: bfloat16 [2048, 2048], P('fsdp'), may hold values from -0.125 to 0.125
- value_weight: bfloat16 [2048, 2048], P('fsdp'), may hold values from -0.125 to 0.125
- out_weight: bfloat16 [2048, 2048], P('fsdp'), may hold values from -0.125 to 0.125
- gate_weight: bfloat16 [2048, 5632], P('fsdp'), may hold values from -0.125 to 0.125
- up_weight: bfloat16 [2048, 5632], P('fsdp'), may hold values from -0.125 to 0.125
- down_weight: bfloat16 [5632, 2048], P('fsdp'), may hold values from -0.078125 to 0.078125
- query_gain: bfloat16 [2048], P('fsdp'), may hold values from 0.5 to 1.5
- key_gain: bfloat16 [2048], P('fsdp'), may hold values from 0.5 to 1.5
- attention_gain: bfloat16 [2048], P('fsdp'), may hold values from 0.5 to 1.5
- feed_gain: bfloat16 [2048], P('fsdp'), may hold values from 0.5 to 1.5
- pair_table: int32 [8, 2], replicated, may hold values from 0 to 15, as said below
Outputs:
- result: bfloat16 [16, 1024, 2048], P('fsdp', 'ctx')
- input_grad: float32 [16, 1024, 2048], P('fsdp', 'ctx')
- query_weight_grad: float32 [2048, 2048], P('fsdp')
- key_weight_grad: float32 [2048, 2048], P('fsdp')
- value_weight_grad: float32 [2048, 2048], P('fsdp')
- out_weight_grad: float32 [2048, 2048], P('fsdp')
- gate_weight_grad: float32 [2048, 5632], P('fsdp')
- up_weight_grad: float32 [2048, 5632], P('fsdp')
- down_weight_grad: float32 [5632, 2048], P('fsdp')
- query_gain_grad: float32 [2048], P('fsdp')
- key_gain_grad: float32 [2048], P('fsdp')
- attention_gain_grad: float32 [2048], P('fsdp')
- feed_gain_grad: float32 [2048], P('fsdp')
Inputs may be any that keep to these rules, and one draw needn't show every extreme that they name: `pair_table`: row r holds a block p and then block 2 n - 1 - p, n the rows of the table; the values p of the rows are a permutation of 0 to n - 1.
All inputs are finite; a program needn't handle non-finite values.
Results may differ from a plain program's by a relative error of at most 0.028.
Values may be sent and summed in bfloat16 or wider, within the bound.
A program may use at most 896 MiB of HBM per device.

v0:
```python
import types

import jax
import jax.numpy as jnp
from jax import lax
from jax.experimental import pallas as pl
from jax.experimental.pallas import tpu as pltpu
from jax.sharding import PartitionSpec as P

HD = 64
EPSILON = 1e-06
THETA = 500000.0
MESH = pl.DeviceIdType.MESH
F32 = jnp.float32
BF16 = jnp.bfloat16
ROOM = 56 * 2**20
NEG = -1e30


def angles(positions):
    freqs = THETA ** (-jnp.arange(0, HD, 2, dtype=F32) / HD)
    phase = positions.astype(F32)[:, None] * jnp.tile(freqs, 4)[None, :]
    return jnp.cos(phase), jnp.sin(phase)


def dot(left, right):
    return jnp.dot(left, right, preferred_element_type=F32)


def outer_sum(left, right):
    return lax.dot_general(left, right, (((0,), (0,)), ((), ())), preferred_element_type=F32)


def back_dot(grad, weight):
    return lax.dot_general(grad, weight, (((1,), (1,)), ((), ())), preferred_element_type=F32)


def low(values):
    return values.astype(BF16)


class Group:
    def __init__(self, axis):
        me = lax.axis_index(axis)
        self.axis = axis
        self.size = lax.axis_size(axis)
        self.me = me
        if axis == "ctx":
            self.core, self.pair, self.place = 0, me // 4, lax.rem(me, 4)
        else:
            self.core, self.pair, self.place = lax.rem(me, 2), lax.rem(me, 4) // 2, me // 4
        self.sibling = me + 1 - 2 * self.core if axis == "fsdp" else None
        self.right, self.left, self.partner = self.at(False, 1), self.at(False, 3), self.at(True, 0)

    def at(self, other, step):
        pair = 1 - self.pair if other else self.pair
        place = lax.rem(self.place + step, 4)
        if self.axis == "ctx":
            return pair * 4 + place
        return place * 4 + pair * 2 + self.core

    def peers(self):
        near = [self.right, self.left, self.partner]
        if self.sibling is not None:
            near.append(self.sibling)
        return [{self.axis: peer} for peer in near]


def meet(peers):
    barrier = pltpu.get_barrier_semaphore()
    for peer in peers:
        pl.semaphore_signal(barrier, inc=1, device_id=peer, device_id_type=MESH)
    pl.semaphore_wait(barrier, len(peers))


class Copies:
    def __init__(self, sent, came):
        self.sent, self.came, self.count, self.all = sent, came, 0, []

    def start(self, src, dst, peer):
        copy = pltpu.make_async_remote_copy(
            src_ref=src,
            dst_ref=dst,
            send_sem=self.sent.at[self.count],
            recv_sem=self.came.at[self.count],
            device_id=peer,
            device_id_type=MESH,
        )
        self.count += 1
        self.all.append(copy)
        copy.start()
        return copy

    def drain(self):
        for copy in self.all:
            copy.wait_send()


class Once:
    def __init__(self, copy):
        self.copy, self.waited = copy, False

    def wait(self):
        if not self.waited:
            self.copy.wait()
        self.waited = True


class Stores:
    def __init__(self, sems):
        self.sems, self.count, self.all = sems, 0, []

    def start(self, src, dst):
        copy = pltpu.make_async_copy(src, dst, self.sems.at[self.count])
        self.count += 1
        copy.start()
        copy = Once(copy)
        self.all.append(copy)
        return copy

    def drain(self):
        for copy in self.all:
            copy.wait()
        self.all = []


def rows_at(index, size):
    return pl.ds(pl.multiple_of(index * size, size), size)


class Rows:
    def __init__(self, ref, blocks):
        self.ref, self.rows = ref, ref.shape[0] // blocks

    def block(self, index, low_row=0, high_row=None):
        high_row = self.rows if high_row is None else high_row
        start = pl.multiple_of(index * self.rows + low_row, 16)
        return self.ref.at[pl.ds(start, high_row - low_row)]


class Strips:
    def __init__(self, ref, blocks):
        self.ref, self.rows, self.width = ref, ref.shape[0], ref.shape[1] // blocks

    def block(self, index, low_row=0, high_row=None):
        high_row = self.rows if high_row is None else high_row
        return self.ref.at[pl.ds(low_row, high_row - low_row), rows_at(index, self.width)]


def arrived(copies):
    for copy in copies:
        copy.wait_recv()


class Cuts:
    def __init__(self, rows, edged):
        half = rows // 2
        start = rows // 8 // 16 * 16 if edged else 0
        stop = rows - rows // 4 // 16 * 16 if edged else rows
        self.all, self.first, self.second = [(0, rows)], [(0, half)], [(half, rows)]
        self.middle = [(start, stop)]
        self.middle_first, self.middle_second = [(start, half)], [(half, stop)]
        self.top = [(0, start)] if start else []
        self.bottom = [(stop, rows)] if stop < rows else []
        self.edges = self.top + self.bottom
        self.half = half


def ring_gather(group, copies, items, edged=False):
    at = group.at
    right, left, partner = ({group.axis: peer} for peer in (group.right, group.left, group.partner))

    def move(index, part, peer, own=False):
        started = []
        for mine, whole in items:
            for lo, hi in getattr(Cuts(whole.rows, edged), part):
                view = whole.block(index, lo, hi)
                started.append(copies.start(mine if own else view, view, peer))
        return started

    near_left = move(group.me, "all", right, True)
    near_right = move(group.me, "all", left, True)
    across = move(group.me, "all", partner, True)
    yield [group.me]
    arrived(near_left)
    far_left = move(group.left, "first", right)
    edges = move(group.left, "edges", partner)
    arrived(near_right)
    far_right = move(group.right, "second", left)
    edges += move(group.right, "edges", partner)
    arrived(across)
    other_left = move(group.partner, "middle", right)
    other_right = move(group.partner, "middle", left)
    yield [group.left, group.right, group.partner]
    arrived(far_left)
    last = move(at(False, 2), "top", partner)
    arrived(far_right)
    last += move(at(False, 2), "bottom", partner)
    yield [at(False, 2)]
    arrived(other_left)
    last += move(at(True, 3), "middle_first", right)
    arrived(other_right)
    last += move(at(True, 1), "middle_second", left)
    arrived(edges)
    yield [at(True, 3), at(True, 1)]
    arrived(last)
    yield [at(True, 2)]


def add(ref, others):
    value = ref[...].astype(F32)
    for other in others:
        value += other[...].astype(F32)
    ref[...] = low(value)


class Sum:
    def __init__(self, parts, far, side, cross, out=None):
        self.parts, self.far, self.side, self.cross, self.out = parts, far, side, cross, out

    def total(self, group):
        own = self.parts.block(group.me)[...].astype(F32)
        sides = self.side[0, 1].astype(F32) + self.side[1, 1].astype(F32)
        return own + sides + self.cross[0].astype(F32)


def landing(rows, columns, edged=False):
    return [
        pltpu.VMEM((2, 2, rows // 2, columns), BF16),
        pltpu.VMEM((2, 2, rows, columns), BF16),
        pltpu.VMEM((4 if edged else 1, rows, columns), BF16),
    ]


def ring_scatter(group, copies, items, prepare, edged=False):
    at = group.at
    right, left, partner = ({group.axis: peer} for peer in (group.right, group.left, group.partner))
    cuts = [Cuts(item.parts.rows, edged) for item in items]

    def window(ref, lead, lo, hi):
        return ref.at[(*lead, pl.ds(lo, hi - lo))]

    def send_edges(step):
        started = []
        for item, cut in zip(items, cuts):
            for lo, hi in cut.edges:
                view = item.parts.block(at(True, step), lo, hi)
                started.append(copies.start(view, window(item.cross, (step,), lo, hi), partner))
        return started

    def add_edges(step):
        for item, cut in zip(items, cuts):
            for lo, hi in cut.edges:
                add(item.parts.block(at(False, step), lo, hi), [window(item.cross, (step,), lo, hi)])

    def far_cut(cut, i, side):
        if side == 0:
            return (cut.middle_first if i == 0 else cut.first)[0]
        return (cut.middle_second if i == 0 else cut.second)[0]

    def far_window(item, cut, i, side):
        lo, hi = far_cut(cut, i, side)
        base = side * cut.half
        return window(item.far, (side, i), lo - base, hi - base)

    def send_far(i):
        started = ([], [])
        for item, cut in zip(items, cuts):
            for side, peer in enumerate((right, left)):
                view = item.parts.block(at(i == 0, 2), *far_cut(cut, i, side))
                started[side].append(copies.start(view, far_window(item, cut, i, side), peer))
        return started

    def send_near(i, far):
        started = []
        for side, (step, peer) in enumerate(((1, right), (3, left))):
            arrived(far[side])
            index = at(i == 0, step)
            for item, cut in zip(items, cuts):
                add(
                    item.parts.block(index, *far_cut(cut, i, side)),
                    [far_window(item, cut, i, side)],
                )
                lo, hi = (cut.middle if i == 0 else cut.all)[0]
                view = item.parts.block(index, lo, hi)
                started.append(copies.start(view, window(item.side, (side, i), lo, hi), peer))
        return started

    prepare(True, 2)
    far_other = send_far(0)
    edges = {2: send_edges(2)}
    yield
    prepare(False, 2)
    arrived(edges[2])
    add_edges(2)
    far_same = send_far(1)
    yield
    for step in (1, 3):
        prepare(True, step)
        edges[step] = send_edges(step)
    yield
    near_other = send_near(0, far_other)
    yield
    prepare(True, 0)
    edges[0] = send_edges(0)
    for step in (1, 3):
        prepare(False, step)
        arrived(edges[step])
        add_edges(step)
    near_same = send_near(1, far_same)
    yield
    arrived(near_other)
    across = []
    for item, cut in zip(items, cuts):
        lo, hi = cut.middle[0]
        view = item.parts.block(group.partner, lo, hi)
        add(view, [window(item.side, (0, 0), lo, hi), window(item.side, (1, 0), lo, hi)])
        across.append(copies.start(view, window(item.cross, (0,), lo, hi), partner))
    yield
    prepare(False, 0)
    yield
    arrived(near_same)
    arrived(across)
    arrived(edges[0])
    yield


def owner_gather(owner, copies, stores, items):
    sibling = {owner.axis: owner.sibling}
    passed, own = [], True
    for mine, whole in items:
        stores.start(mine, whole.block(owner.me))
    for indexes in ring_gather(owner, copies, items):
        for index in indexes:
            for mine, whole in items:
                view = whole.block(index)
                passed.append(copies.start(mine if own else view, view, sibling))
        own = False
        yield
    arrived(passed)
    yield


def owner_sum(owner, copies, stores, sources, sums, from_sibling):
    sibling = {owner.axis: owner.sibling}
    turn = 1 - 2 * owner.core
    waits = {}
    for step in (2, 1, 3, 0):
        for other in (True, False):
            index, number = owner.at(other, step), len(waits)
            waits[other, step] = [
                (
                    stores.start(source.block(index), item.parts.block(index)),
                    copies.start(source.block(index + turn), landed.at[number], sibling),
                    landed.at[number],
                )
                for source, item, landed in zip(sources, sums, from_sibling)
            ]

    def prepare(other, step):
        for (fetch, give, landed), item in zip(waits[other, step], sums):
            fetch.wait()
            give.wait_recv()
            add(item.parts.block(owner.at(other, step)), [landed])

    yield from ring_scatter(owner, copies, sums, prepare)
    for item in sums:
        item.out[...] = low(item.total(owner))
    yield


def sum_scratch(rows, columns, owners):
    return [
        pltpu.VMEM((owners * rows, columns), BF16),
        pltpu.VMEM((owners // 2, rows, columns), BF16),
        *landing(rows, columns),
    ]


FAR = pl.BlockSpec(memory_space=pl.ANY)
NEAR = pl.BlockSpec(memory_space=pltpu.VMEM)


def shape(dims, kind=BF16):
    return jax.ShapeDtypeStruct(dims, kind)


def launch(number, body, ins, outs, temps, remote, local):
    names, scratch, groups = [*ins, *outs], [], []
    for name, kind in temps.items():
        kinds = kind if isinstance(kind, list) else [kind]
        groups.append((name, len(kinds), isinstance(kind, list)))
        scratch += kinds
    dma = pltpu.SemaphoreType.DMA
    scratch += [dma((remote,)), dma((remote,)), dma((local,))]

    def kernel(*refs):
        named = dict(zip(names, refs))
        rest = list(refs[len(names) :])
        for name, count, many in groups:
            named[name] = rest[:count] if many else rest[0]
            del rest[:count]
        sent, came, near = rest
        body(types.SimpleNamespace(**named), Copies(sent, came), Stores(near))

    results = pl.pallas_call(
        kernel,
        out_shape=[out for out, _ in outs.values()],
        in_specs=[spec for _, spec in ins.values()],
        out_specs=[spec for _, spec in outs.values()],
        scratch_shapes=scratch,
        compiler_params=pltpu.CompilerParams(
            collective_id=number, has_side_effects=True, vmem_limit_bytes=ROOM
        ),
    )(*[array for array, _ in ins.values()])
    return types.SimpleNamespace(**dict(zip(outs, results)))


def near(**arrays):
    return {name: (array, NEAR) for name, array in arrays.items()}


def far(**arrays):
    return {name: (array, FAR) for name, array in arrays.items()}


def tiles(product, rows, value, weight, tile, transposed):
    def step(i, carry):
        span = rows_at(i, tile)
        if transposed:
            piece = back_dot(value, weight[span, :])
        else:
            piece = dot(value, weight[:, span])
        product[rows, span] = piece.astype(product.dtype)
        return carry

    lax.fori_loop(0, product.shape[1] // tile, step, 0)


def totals_by_row(select, value):
    return lax.dot_general(
        select,
        value,
        (((1,), (1,)), ((), ())),
        precision=lax.Precision.HIGHEST,
        preferred_element_type=F32,
    )


class Gathered:
    def __init__(self, group, copies, stores, block, landed, whole, use):
        self.group, self.stores, self.use = group, stores, use
        self.block, self.landed = block, Rows(landed, group.size)
        self.whole = Rows(whole, group.size)
        self.stream = ring_gather(group, copies, [(block, self.landed)], True)
        self.ready, self.fresh = [], True

    def step(self):
        self.ready += [(self.fresh, index) for index in next(self.stream)]
        self.fresh = False

    def consume(self):
        for own, index in self.ready:
            src = self.block if own else self.landed.block(index)
            self.stores.start(src, self.whole.block(index))
            self.use(src, index)
        self.ready = []


def gathered_all(gathered, pump):
    gathered.consume()
    for _ in range(4):
        pump()
        gathered.step()
        gathered.consume()


def ctx_sum(group, copies, act, weight, item, tile, transposed):
    parts = item.parts

    def prepare(other, step):
        rows = rows_at(group.at(other, step), parts.rows)
        tiles(parts.ref, rows, act[rows, :], weight, tile, transposed)

    return ring_scatter(group, copies, [item], prepare, True)


def weave(main, stream):
    for _ in main:
        if stream is not None:
            next(stream, None)


def finish(stream):
    for _ in stream:
        pass


def norm(values):
    inverse = lax.rsqrt(jnp.mean(values * values, axis=-1, keepdims=True) + EPSILON)
    return values * inverse, inverse


def norm_back(grad, unit, inverse, gain):
    pull = grad * gain
    return inverse * (pull - unit * jnp.mean(pull * unit, axis=-1, keepdims=True))


def head_lanes(shape):
    return lax.broadcasted_iota(jnp.int32, shape, 1) < HD


def turn_lanes(shape):
    return lax.rem(lax.broadcasted_iota(jnp.int32, shape, 1), HD) < HD // 2


def turned(values):
    lanes = values.shape[1]
    ahead = pltpu.roll(values, lanes - HD // 2, 1)
    behind = pltpu.roll(values, HD // 2, 1)
    return jnp.where(turn_lanes(values.shape), -ahead, behind)


def turned_back(values):
    lanes = values.shape[1]
    ahead = pltpu.roll(values, lanes - HD // 2, 1)
    behind = pltpu.roll(values, HD // 2, 1)
    return jnp.where(turn_lanes(values.shape), ahead, -behind)


def soft(keys, query, key_pos, query_pos):
    scores = back_dot(keys, query) * HD ** (-0.5)
    scores = jnp.where(query_pos >= key_pos, scores, NEG)
    expo = jnp.exp(scores - jnp.max(scores, axis=0, keepdims=True))
    return expo / jnp.sum(expo, axis=0, keepdims=True)


def heads_of(query):
    first = head_lanes(query.shape)
    return first, jnp.logical_not(first)


def pair_of(outs):
    return jnp.concatenate([outs[0][:HD], outs[1][HD:]], axis=0)


def attend(block, qkv_mine, gains_mine, out_mine, gate_up_mine, cosine, sine, positions, number):
    ranks, owners = lax.axis_size("ctx"), lax.axis_size("fsdp")
    (size, depth), columns = block.shape, qkv_mine.shape[1]
    length, share, chunk = ranks * size, columns // 3, 256
    lanes = 2 * HD

    def body(r, copies, stores):
        group, owner = Group("ctx"), Group("fsdp")
        others = [{"ctx": lax.rem(group.me + step, ranks)} for step in range(1, ranks)]
        meet(others + owner.peers())
        normed = 2 * share
        by_lane = lax.broadcasted_iota(jnp.int32, (8, normed), 1) < share
        by_row = lax.broadcasted_iota(jnp.int32, (8, normed), 0) < 4
        select = jnp.where(by_lane == by_row, 1.0, 0.0)

        def use(src, index):
            rows = rows_at(index, size)
            tiles(r.proj, rows, src[...], r.qkv_near, 256, False)
            value = r.proj[rows, pl.ds(0, normed)]
            r.sums[:, rows] = totals_by_row(select, value * value)

        gathered = Gathered(group, copies, stores, r.block, r.landed, r.whole, use)
        gains_all = Rows(r.gains_near, owners)
        first = owner_gather(
            owner,
            copies,
            stores,
            [(r.qkv_mine, Rows(r.qkv_near, owners)), (r.gains_mine, gains_all)],
        )
        second = owner_gather(
            owner,
            copies,
            stores,
            [
                (r.out_mine, Strips(r.out_near, owners)),
                (r.gate_up_mine, Rows(r.gate_up_near, owners)),
            ],
        )
        next(first)
        gathered.step()
        next(first)
        next(first)
        next(first)
        next(second)
        gathered.step()
        finish(first)
        stores.drain()
        stores.start(r.qkv_near, r.qkv)
        gathered.consume()
        for _ in range(3):
            next(second)
            gathered.step()
            gathered.consume()
        exchange = [copies.start(r.sums, r.sums_landed.at[i], to) for i, to in enumerate(others)]
        for i in range(owners):
            rows = r.gains_near[pl.ds(i * gains_all.rows, 16), :].astype(F32)
            r.scales[:, pl.ds(i * rows.shape[1], rows.shape[1])] = rows[:8]
        arrived(exchange)
        totals = r.sums[...] + jnp.sum(r.sums_landed[...], axis=0)
        r.inverse[...] = lax.rsqrt(totals * (1.0 / (ranks * share)) + EPSILON).T
        mine = rows_at(group.me, share)
        for i, (unit, out) in enumerate(((r.query_unit, r.queries), (r.key_unit, r.keys))):
            span = pl.ds(i * share, share)
            unit[...] = r.proj[:, span] * r.inverse[:, 4 * i : 4 * i + 1]
            gain = r.scales[i : i + 1, mine]
            for pair in range(share // lanes):
                part = pl.ds(pair * lanes, lanes)
                scaled = unit[:, part] * gain[:, pair * lanes : (pair + 1) * lanes]
                out[:, part] = low(scaled * r.cosine[...] + turned(scaled) * r.sine[...])
        r.values[...] = low(r.proj[:, pl.ds(2 * share, share)])

        for pair in range(share // lanes):
            span = pl.ds(pair * lanes, lanes)
            value_turned = r.values[:, span].astype(F32).T.astype(BF16)

            def step(i, carry):
                rows = rows_at(i, chunk)
                query = r.queries[rows, span]
                nothing = jnp.zeros_like(query)
                outs = []
                for mask in heads_of(query):
                    query_head = jnp.where(mask, query, nothing)
                    probs = soft(r.keys[:, span], query_head, r.key_pos[...], r.query_pos[:, rows])
                    outs.append(dot(value_turned, low(probs)))
                r.mixed[rows, span] = low(pair_of(outs).T)
                return carry

            steps = length // chunk
            lax.fori_loop(0, steps // 2, step, 0)
            next(second, None)
            lax.fori_loop(steps // 2, steps, step, 0)
            next(second, None)
        finish(second)
        stores.drain()
        stores.start(r.out_near, r.out_rows)
        stores.start(r.gate_up_near, r.gate_up)
        stores.drain()
        copies.drain()

    return launch(
        number,
        body,
        near(
            block=block,
            qkv_mine=qkv_mine,
            gains_mine=gains_mine,
            out_mine=out_mine,
            gate_up_mine=gate_up_mine,
            cosine=cosine,
            sine=sine,
            key_pos=positions[:, None],
            query_pos=positions[None, :],
        ),
        far(
            whole=shape((length, depth)),
            qkv=shape((depth, columns)),
            out_rows=shape((share, depth)),
            gate_up=shape((depth, gate_up_mine.shape[1])),
        )
        | near(
            scales=shape((8, depth), F32),
            inverse=shape((length, 8), F32),
            query_unit=shape((length, share), F32),
            key_unit=shape((length, share), F32),
            queries=shape((length, share)),
            keys=shape((length, share)),
            values=shape((length, share)),
            mixed=shape((length, share)),
        ),
        dict(
            landed=pltpu.VMEM((length, depth), BF16),
            qkv_near=pltpu.VMEM((depth, columns), BF16),
            gains_near=pltpu.VMEM((owners * gains_mine.shape[0], gains_mine.shape[1]), BF16),
            out_near=pltpu.VMEM((share, depth), BF16),
            gate_up_near=pltpu.VMEM((depth, gate_up_mine.shape[1]), BF16),
            proj=pltpu.VMEM((length, columns), F32),
            sums=pltpu.VMEM((8, length), F32),
            sums_landed=pltpu.VMEM((ranks - 1, 8, length), F32),
        ),
        15 + 34 + 34 + ranks - 1,
        20,
    )


def feed_in(mixed, out_rows, block, scales, gate_up, down_mine, number):
    ranks, owners = lax.axis_size("ctx"), lax.axis_size("fsdp")
    size, width = block.shape
    length, both = mixed.shape[0], gate_up.shape[1]
    room = both // 2

    def body(r, copies, stores):
        group, owner = Group("ctx"), Group("fsdp")
        fetches = [
            stores.start(r.mixed, r.act),
            stores.start(r.out_rows, r.out_near),
            stores.start(r.gate_up, r.gate_up_near),
        ]
        meet(group.peers() + owner.peers())
        item = Sum(Rows(r.part, ranks), *r.landings)
        fetches[0].wait()
        fetches[1].wait()
        summed = ctx_sum(group, copies, r.act, r.out_near, item, 512, False)
        down = owner_gather(
            owner, copies, stores, [(r.down_mine, Strips(r.down_near, owners))]
        )
        next(summed)
        weave(summed, down)
        attn_raw = item.total(group)
        r.attn_raw[...] = attn_raw
        unit, _ = norm(attn_raw)
        hidden = r.block[...].astype(F32) + unit * r.scales[2:3, :]
        r.hidden[...] = hidden
        r.hidden_low[...] = low(hidden)
        fetches[2].wait()

        def use(src, index):
            rows = rows_at(index, size)
            tiles(r.pre_near, rows, src[...], r.gate_up_near, 512, False)
            stores.start(r.pre_near.at[rows], r.pre.at[rows])
            gate, up = r.pre_near[rows, pl.ds(0, room)], r.pre_near[rows, pl.ds(room, room)]
            r.product[rows, :] = low(gate * jax.nn.sigmoid(gate) * up)

        gathered = Gathered(group, copies, stores, r.hidden_low, r.landed, r.whole, use)
        gathered.step()
        gathered_all(gathered, lambda: next(down, None))
        finish(down)
        stores.drain()
        stores.start(r.down_near, r.down_rows).wait()
        copies.drain()

    return launch(
        number,
        body,
        far(mixed=mixed, out_rows=out_rows, gate_up=gate_up)
        | near(block=block, scales=scales, down_mine=down_mine),
        far(
            whole=shape((length, width)),
            pre=shape((length, both), F32),
            down_rows=shape((room, width)),
        )
        | near(
            attn_raw=shape((size, width), F32),
            hidden=shape((size, width), F32),
            product=shape((length, room)),
        ),
        dict(
            act=pltpu.VMEM(mixed.shape, BF16),
            out_near=pltpu.VMEM(out_rows.shape, BF16),
            gate_up_near=pltpu.VMEM(gate_up.shape, BF16),
            down_near=pltpu.VMEM((room, width), BF16),
            part=pltpu.VMEM((length, width), BF16),
            landings=landing(size, width, True),
            landed=pltpu.VMEM((length, width), BF16),
            hidden_low=pltpu.VMEM((size, width), BF16),
            pre_near=pltpu.VMEM((length, both), F32),
        ),
        17 + 15 + 17,
        22,
    )


def feed_out(product, down_rows, pre, hidden, cotangent, scales, number):
    ranks = lax.axis_size("ctx")
    size, width = hidden.shape
    length, both = pre.shape
    room = both // 2

    def body(r, copies, stores):
        group = Group("ctx")
        fetches = [
            stores.start(r.product, r.act),
            stores.start(r.down_rows, r.down_near),
            stores.start(r.pre, r.pre_near),
        ]
        meet(group.peers())
        item = Sum(Rows(r.part, ranks), *r.landings)
        fetches[0].wait()
        fetches[1].wait()
        finish(ctx_sum(group, copies, r.act, r.down_near, item, 512, False))
        unit, inverse = norm(item.total(group))
        gain = r.scales[3:4, :]
        r.result[...] = low(r.hidden[...] + unit * gain)
        upstream = r.cotangent[...].astype(F32)
        r.feed_term[...] = jnp.sum(upstream * unit, axis=0, keepdims=True)
        r.down_low[...] = low(norm_back(upstream, unit, inverse, gain))
        fetches[2].wait()

        def use(src, index):
            rows = rows_at(index, size)
            tiles(r.product_grad, pl.ds(0, size), src[...], r.down_near, 256, True)
            gate, up = r.pre_near[rows, pl.ds(0, room)], r.pre_near[rows, pl.ds(room, room)]
            grad, sigmoid = r.product_grad[...], jax.nn.sigmoid(gate)
            r.both_low[rows, pl.ds(0, room)] = low(
                grad * up * sigmoid * (1.0 + gate * (1.0 - sigmoid))
            )
            r.both_low[rows, pl.ds(room, room)] = low(grad * gate * sigmoid)

        gathered = Gathered(group, copies, stores, r.down_low, r.landed, r.whole, use)
        gathered.step()
        gathered_all(gathered, lambda: None)
        stores.drain()
        copies.drain()

    return launch(
        number,
        body,
        far(product=product, down_rows=down_rows, pre=pre)
        | near(hidden=hidden, cotangent=cotangent, scales=scales),
        far(whole=shape((length, width)))
        | near(
            result=shape((size, width)),
            feed_term=shape((1, width), F32),
            both_low=shape((length, both)),
        ),
        dict(
            act=pltpu.VMEM(product.shape, BF16),
            down_near=pltpu.VMEM(down_rows.shape, BF16),
            pre_near=pltpu.VMEM((length, both), F32),
            part=pltpu.VMEM((length, width), BF16),
            landings=landing(size, width, True),
            landed=pltpu.VMEM((length, width), BF16),
            down_low=pltpu.VMEM((size, width), BF16),
            product_grad=pltpu.VMEM((size, room), F32),
        ),
        17 + 15,
        12,
    )


def hidden_back(
    both_low, gate_up, cotangent, attn_raw, scales, out_rows, gate_up_grad, down_grad, number
):
    ranks, owners = lax.axis_size("ctx"), lax.axis_size("fsdp")
    size, width = attn_raw.shape
    length, both = both_low.shape
    share = out_rows.shape[0]
    gate_up_block = (gate_up_grad.shape[0] // owners, both)
    down_block = (down_grad.shape[0], width // owners)

    def body(r, copies, stores):
        group, owner = Group("ctx"), Group("fsdp")
        fetches = [
            stores.start(r.both_low, r.act),
            stores.start(r.gate_up, r.gate_up_near),
            stores.start(r.out_rows, r.out_near),
        ]
        meet(group.peers() + owner.peers())
        item = Sum(Rows(r.part, ranks), *r.landings)
        owned = []
        for grad, out, scratch in (
            (Rows(r.gate_up_grad, owners), r.gate_up_share, r.gate_up_sum),
            (Strips(r.down_grad, owners), r.down_share, r.down_sum),
        ):
            part, from_sibling, *places = scratch
            own = Sum(Rows(part, owners), *places, out)
            owned.append(owner_sum(owner, copies, stores, [grad], [own], [from_sibling]))
        next(owned[0])
        fetches[0].wait()
        fetches[1].wait()
        weave(ctx_sum(group, copies, r.act, r.gate_up_near, item, 512, True), owned[0])
        hidden_grad = r.cotangent[...].astype(F32) + item.total(group)
        r.hidden_grad[...] = hidden_grad
        unit, inverse = norm(r.attn_raw[...])
        r.attn_term[...] = jnp.sum(hidden_grad * unit, axis=0, keepdims=True)
        r.attn_low[...] = low(norm_back(hidden_grad, unit, inverse, r.scales[2:3, :]))
        fetches[2].wait()

        def use(src, index):
            tiles(r.mixed_grad, rows_at(index, size), src[...], r.out_near, 256, True)

        gathered = Gathered(group, copies, stores, r.attn_low, r.landed, r.whole, use)
        gathered.step()
        finish(owned[0])

        def pump():
            next(owned[1], None)
            next(owned[1], None)

        gathered_all(gathered, pump)
        finish(owned[1])
        stores.drain()
        copies.drain()

    return launch(
        number,
        body,
        far(
            both_low=both_low,
            gate_up=gate_up,
            out_rows=out_rows,
            gate_up_grad=gate_up_grad,
            down_grad=down_grad,
        )
        | near(cotangent=cotangent, attn_raw=attn_raw, scales=scales),
        far(whole=shape((length, width)))
        | near(
            hidden_grad=shape((size, width), F32),
            attn_term=shape((1, width), F32),
            mixed_grad=shape((length, share)),
            gate_up_share=shape(gate_up_block),
            down_share=shape(down_block),
        ),
        dict(
            act=pltpu.VMEM(both_low.shape, BF16),
            gate_up_near=pltpu.VMEM(gate_up.shape, BF16),
            out_near=pltpu.VMEM(out_rows.shape, BF16),
            part=pltpu.VMEM((length, width), BF16),
            landings=landing(size, width, True),
            landed=pltpu.VMEM((length, width), BF16),
            attn_low=pltpu.VMEM((size, width), BF16),
            gate_up_sum=sum_scratch(*gate_up_block, owners),
            down_sum=sum_scratch(*down_block, owners),
        ),
        17 + 15 + 17 + 17,
        3 + 8 + 8 + 8,
    )


def attend_back(front, mixed_grad, cosine, sine, positions, gate_up_share, number):
    ranks = lax.axis_size("ctx")
    length, share = mixed_grad.shape
    lanes, chunk = 2 * HD, 256
    whole = (ranks * gate_up_share.shape[0], gate_up_share.shape[1])

    def body(r, copies, stores):
        group = Group("ctx")
        others = [{"ctx": lax.rem(group.me + step, ranks)} for step in range(1, ranks)]
        meet(others)
        all_shares, stored = Rows(r.landed, ranks), Rows(r.whole, ranks)
        stream = ring_gather(group, copies, [(r.block, all_shares)], True)
        next(stream)
        stores.start(r.block, stored.block(group.me))
        r.key_turn[...] = jnp.zeros_like(r.key_turn)
        r.value_sum[...] = jnp.zeros_like(r.value_sum)

        def advance():
            for index in next(stream, []):
                stores.start(all_shares.block(index), stored.block(index))

        for pair in range(share // lanes):
            span = pl.ds(pair * lanes, lanes)
            key_turned = r.keys[:, span].astype(F32).T.astype(BF16)

            def step(i, carry):
                rows = rows_at(i, chunk)
                query, grad = r.queries[rows, span], r.mixed_grad[rows, span]
                nothing = jnp.zeros_like(query)
                outs = []
                for mask in heads_of(query):
                    query_head = jnp.where(mask, query, nothing)
                    grad_head = jnp.where(mask, grad, nothing)
                    probs = soft(r.keys[:, span], query_head, r.key_pos[...], r.query_pos[:, rows])
                    prob_grad = back_dot(r.values[:, span], grad_head)
                    delta = jnp.sum(probs * prob_grad, axis=0, keepdims=True)
                    score_low = low(probs * (prob_grad - delta))
                    r.value_sum[:, span] += dot(low(probs), grad_head)
                    r.key_turn[:, span] += dot(score_low, query_head)
                    outs.append(dot(key_turned, score_low))
                query_rot = (pair_of(outs) * HD ** (-0.5)).T
                r.query_turn[rows, span] = query_rot * r.cosine[rows, :] + turned_back(
                    query_rot * r.sine[rows, :]
                )
                return carry

            steps = length // chunk
            lax.fori_loop(0, steps // 2, step, 0)
            advance()
            lax.fori_loop(steps // 2, steps, step, 0)
            advance()
            key_rot = r.key_turn[:, span] * HD ** (-0.5)
            r.key_turn[:, span] = key_rot * r.cosine[...] + turned_back(key_rot * r.sine[...])
        by_row = lax.broadcasted_iota(jnp.int32, (8, share), 0) < 4
        mine = rows_at(group.me, share)
        for i, (turn, unit) in enumerate(
            ((r.query_turn, r.query_unit), (r.key_turn, r.key_unit))
        ):
            product = turn[...] * unit[...]
            r.terms[pl.ds(i, 1), :] = jnp.sum(product, axis=0, keepdims=True)
            part = totals_by_row(
                jnp.where(by_row == (i == 0), 1.0, 0.0), product * r.scales[i : i + 1, mine]
            )
            r.sums[...] = part if i == 0 else r.sums[...] + part
        exchange = [copies.start(r.sums, r.sums_landed.at[i], to) for i, to in enumerate(others)]
        arrived(exchange)
        totals = r.sums[...] + jnp.sum(r.sums_landed[...], axis=0)
        means = (totals * (1.0 / (ranks * share))).T
        for i, (turn, unit) in enumerate(
            ((r.query_turn, r.query_unit), (r.key_turn, r.key_unit))
        ):
            column = slice(4 * i, 4 * i + 1)
            r.qkv_low[:, pl.ds(i * share, share)] = low(
                r.inverse[:, column]
                * (turn[...] * r.scales[i : i + 1, mine] - unit[...] * means[:, column])
            )
        r.qkv_low[:, pl.ds(2 * share, share)] = low(r.value_sum[...])
        for _ in range(5):
            advance()
        copies.drain()
        stores.drain()

    return launch(
        number,
        body,
        near(
            queries=front.queries,
            keys=front.keys,
            values=front.values,
            query_unit=front.query_unit,
            key_unit=front.key_unit,
            inverse=front.inverse,
            scales=front.scales,
            mixed_grad=mixed_grad,
            cosine=cosine,
            sine=sine,
            key_pos=positions[:, None],
            query_pos=positions[None, :],
            block=gate_up_share,
        ),
        near(qkv_low=shape((length, 3 * share)), terms=shape((2, share), F32))
        | far(whole=shape(whole)),
        dict(
            query_turn=pltpu.VMEM((length, share), F32),
            key_turn=pltpu.VMEM((length, share), F32),
            value_sum=pltpu.VMEM((length, share), F32),
            sums=pltpu.VMEM((8, length), F32),
            sums_landed=pltpu.VMEM((ranks - 1, 8, length), F32),
            landed=pltpu.VMEM(whole, BF16),
        ),
        15 + ranks - 1,
        8,
    )


def input_back(qkv_low, qkv, hidden_grad, qkv_grad, strip_grad, number):
    ranks, owners = lax.axis_size("ctx"), lax.axis_size("fsdp")
    size, width = hidden_grad.shape
    length = qkv_low.shape[0]
    qkv_block = (qkv_grad.shape[0] // owners, qkv_grad.shape[1])
    strip_block = (strip_grad.shape[0], width // owners)

    def body(r, copies, stores):
        group, owner = Group("ctx"), Group("fsdp")
        fetches = [stores.start(r.qkv_low, r.act), stores.start(r.qkv, r.qkv_near)]
        meet(group.peers() + owner.peers())
        item = Sum(Rows(r.part, ranks), *r.landings)
        sums = [
            Sum(Rows(scratch[0], owners), *scratch[2:], out)
            for scratch, out in ((r.qkv_sum, r.qkv_share), (r.strip_sum, r.strip_share))
        ]
        owned = owner_sum(
            owner,
            copies,
            stores,
            [Rows(r.qkv_grad, owners), Strips(r.strip_grad, owners)],
            sums,
            [r.qkv_sum[1], r.strip_sum[1]],
        )
        next(owned)
        for fetch in fetches:
            fetch.wait()
        weave(ctx_sum(group, copies, r.act, r.qkv_near, item, 512, True), owned)
        r.input_grad[...] = r.hidden_grad[...] + item.total(group)
        finish(owned)
        copies.drain()

    return launch(
        number,
        body,
        far(qkv_low=qkv_low, qkv=qkv, qkv_grad=qkv_grad, strip_grad=strip_grad)
        | near(hidden_grad=hidden_grad),
        near(
            input_grad=shape((size, width), F32),
            qkv_share=shape(qkv_block),
            strip_share=shape(strip_block),
        ),
        dict(
            act=pltpu.VMEM(qkv_low.shape, BF16),
            qkv_near=pltpu.VMEM(qkv.shape, BF16),
            part=pltpu.VMEM((length, width), BF16),
            landings=landing(size, width, True),
            qkv_sum=sum_scratch(*qkv_block, owners),
            strip_sum=sum_scratch(*strip_block, owners),
        ),
        17 + 34,
        2 + 16,
    )


def spread(parts, number):
    ranks, count = lax.axis_size("ctx"), len(parts)
    wholes = [(ranks * part.shape[0], part.shape[1]) for part in parts]
    names = [f"part_{i}" for i in range(count)]

    def body(r, copies, stores):
        group = Group("ctx")
        meet(group.peers())
        mine = [getattr(r, name) for name in names]
        stored = [Rows(getattr(r, "whole_" + name), ranks) for name in names]
        landed = [Rows(ref, ranks) for ref in r.landed]
        own = True
        for indexes in ring_gather(group, copies, list(zip(mine, landed)), True):
            for index in indexes:
                for block, all_blocks, to in zip(mine, landed, stored):
                    stores.start(block if own else all_blocks.block(index), to.block(index))
                own = False
        copies.drain()
        stores.drain()

    outs = launch(
        number,
        body,
        near(**dict(zip(names, parts))),
        far(**{"whole_" + name: shape(dims) for name, dims in zip(names, wholes)}),
        dict(landed=[pltpu.VMEM(dims, BF16) for dims in wholes]),
        15 * count,
        8 * count,
    )
    return [getattr(outs, "whole_" + name) for name in names]


def body(
    layer_input,
    cotangent,
    query_weight,
    key_weight,
    value_weight,
    out_weight,
    gate_weight,
    up_weight,
    down_weight,
    query_gain,
    key_gain,
    attention_gain,
    feed_gain,
    pair_table,
):
    row_count = layer_input.shape[1]
    block_len = row_count // 2
    rank = lax.axis_index("ctx")
    owner = lax.axis_index("fsdp")
    ranks = lax.axis_size("ctx")
    owners = lax.axis_size("fsdp")
    width = query_weight.shape[1]
    share = width // ranks
    strip = width // owners
    units = gate_weight.shape[1] // ranks
    room = -(-units // 256) * 256
    blocks = pair_table.reshape(-1)
    positions = (
        blocks[:, None] * block_len + jnp.arange(block_len, dtype=jnp.int32)[None, :]
    ).reshape(-1)
    cosine, sine = angles(positions)

    def cut(weight, size):
        return lax.dynamic_slice_in_dim(weight, rank * size, size, axis=1)

    def wide(weight):
        return jnp.pad(cut(weight, units), ((0, 0), (0, room - units)))

    inputs = layer_input[0]
    qkv_mine = jnp.concatenate(
        [cut(w, share) for w in (query_weight, key_weight, value_weight)], axis=1
    )
    gains_mine = jnp.pad(
        jnp.stack([query_gain, key_gain, attention_gain, feed_gain]), ((0, 28), (0, 0))
    )
    flat = lambda c, f: c * owners + f
    odd = lax.rem(owner, 2)
    routes = [
        [
            (flat(c, 2 * d + j), flat(d, 2 * c + (j ^ k)))
            for c in range(ranks)
            for d in range(ranks)
            for j in range(2)
        ]
        for k in range(2)
    ]
    axes = ("ctx", "fsdp")
    tall = jnp.concatenate([out_weight, down_weight], axis=0)
    pieces = []
    for k, route in enumerate(routes):
        target = 2 * rank + (odd ^ k)
        strips = lax.dynamic_slice_in_dim(tall, target * strip, strip, axis=1)
        pieces.append(lax.ppermute(strips, axes, route))

    def in_order(pair):
        return jnp.where(odd == 0, pair[0], pair[1]), jnp.where(odd == 0, pair[1], pair[0])

    low_piece, high_piece = in_order(pieces)
    out_size = out_weight.shape[0]
    strips = jnp.concatenate(
        [
            low_piece[:out_size],
            high_piece[:out_size],
            low_piece[out_size:],
            high_piece[out_size:],
            jnp.zeros((room - units, strip), BF16),
        ],
        axis=0,
    )

    front = attend(
        inputs,
        qkv_mine,
        gains_mine,
        strips[:share],
        jnp.concatenate([wide(gate_weight), wide(up_weight)], axis=1),
        cosine,
        sine,
        positions,
        1,
    )
    fed = feed_in(
        front.mixed, front.out_rows, inputs, front.scales, front.gate_up, strips[share:], 2
    )
    back = feed_out(
        fed.product, fed.down_rows, fed.pre, fed.hidden, cotangent[0], front.scales, 3
    )
    gate_up_grad = low(outer_sum(fed.whole, back.both_low))
    down_grad = low(outer_sum(fed.product, back.whole))
    inner = hidden_back(
        back.both_low,
        front.gate_up,
        cotangent[0],
        fed.attn_raw,
        front.scales,
        front.out_rows,
        gate_up_grad,
        down_grad,
        4,
    )
    out_rows_grad = low(outer_sum(front.mixed, inner.whole))
    outer = attend_back(
        front, inner.mixed_grad, cosine, sine, positions, inner.gate_up_share, 5
    )
    qkv_grad = low(outer_sum(front.whole, outer.qkv_low))

    def placed(term):
        return lax.dynamic_update_slice_in_dim(
            jnp.zeros((width,), F32), term, rank * share, axis=0
        )

    gain_terms = low(jnp.stack([placed(outer.terms[0]), placed(outer.terms[1]), inner.attn_term[0], back.feed_term[0]]))
    strip_grads = jnp.concatenate([out_rows_grad, jnp.pad(gain_terms, ((0, 28), (0, 0)))], axis=0)
    last = input_back(
        outer.qkv_low, front.qkv, inner.hidden_grad, qkv_grad, strip_grads, 6
    )
    out_share, gains_share = last.strip_share[:share], last.strip_share[share:]
    down_share = inner.down_share
    down_size = down_weight.shape[0]
    by_owner = [
        jnp.concatenate(
            [
                out_share[j * out_size : (j + 1) * out_size],
                down_share[j * down_size : (j + 1) * down_size],
            ],
            axis=0,
        )
        for j in range(2)
    ]
    by_route = in_order(by_owner)
    returned = [
        lax.ppermute(piece, axes, [(b, a) for a, b in route])
        for piece, route in zip(by_route, routes)
    ]
    tall_share = jnp.concatenate(in_order(returned), axis=1)

    qkv_all, tall_all, gains_all = spread([last.qkv_share, tall_share, gains_share], 7)

    def side_by_side(parts, size, at):
        columns = parts.reshape(ranks, -1, parts.shape[-1])[:, :, at : at + size]
        return columns.transpose(1, 0, 2).reshape(columns.shape[1], -1).astype(F32)

    gate_share, up_share = (side_by_side(outer.whole, units, at) for at in (0, room))
    query_share, key_share, value_share = (
        side_by_side(qkv_all, share, i * share) for i in range(3)
    )
    tall_whole = side_by_side(tall_all, share, 0)
    out_share, down_share = tall_whole[:out_size], tall_whole[out_size:]

    mine = jnp.sum(gains_all.reshape(ranks, -1, strip)[:, :4].astype(F32), axis=0)
    return (
        back.result[None],
        last.input_grad[None],
        query_share,
        key_share,
        value_share,
        out_share,
        gate_share,
        up_share,
        down_share,
        mine[0],
        mine[1],
        mine[2],
        mine[3],
    )


def solution(mesh):
    weights = (P("fsdp", None),) * 7
    gains = (P("fsdp"),) * 4
    tokens = P("fsdp", "ctx", None)
    in_specs = (tokens, tokens, *weights, *gains, P())
    out_specs = (tokens, tokens, *weights, *gains)
    return jax.shard_map(body, mesh=mesh, in_specs=in_specs, out_specs=out_specs, check_vma=False)
```

profile of v0, /device:TPU:2, one launch (start us, length us, event | category | flops | bytes accessed | tf_op | source)
XLA Modules:
  0.0 531.8 jit_solution(1188463436931638304)
XLA Ops:
  1.9 1.5 constant_dynamic-update-slice_fusion
  3.4 3.8 collective-permute-start
  10.9 3.0 multiply_sine_fusion
  18.8 88.0 %shard_map.237 = (bf16[1024,2048]{1,0:T(8,128)(2,1)}, bf16[2048,768]{1,0:T(8,128)(2,1)}, bf16[256,2048]{1,0:T(8,128)(2,1)}, bf16[2048,1536]{1,0:T(8,128)(2,1)}, ...) custom-call(bf16[128,2048]{1,0:T(8,128)(2,1)} %bitcast.59, ...), custom_call_target="tpu_custom_call" | custom-call | tf_op jit(solution)/shard_map/pallas_call | solution.py:406
  106.8 74.5 %shard_map.238 = (bf16[1024,2048]{1,0:T(8,128)(2,1)}, f32[1024,1536]{1,0:T(8,128)}, bf16[768,2048]{1,0:T(8,128)(2,1)}, f32[128,2048]{1,0:T(8,128)}, f32[128,2048]{1,0:T(8,128)}, /*index=5*/bf16[1024,768]{1,0:T(8,128)(2,1)}) custom-call(bf16[1024,256]{1,0:T(8,128)(2,1)} %get-tuple-element.50.refs_0_, bf16[256,2048]{1,0:T(8,128)(2,1)} %get-tuple-element.51.refs_1_.refs_2_, ...), custom_call_target="tpu_custom_call" | custom-call | tf_op jit(solution)/shard_map/pallas_call | solution.py:406
  181.3 72.3 %shard_map.239 = (bf16[1024,2048]{1,0:T(8,128)(2,1)}, bf16[128,2048]{1,0:T(8,128)(2,1)}, f32[1,2048]{1,0:T(1,128)}, bf16[1024,1536]{1,0:T(8,128)(2,1)}) custom-call(bf16[1024,768]{1,0:T(8,128)(2,1)} %get-tuple-element.54.refs_0_, bf16[768,2048]{1,0:T(8,128)(2,1)} %get-tuple-element.55.refs_1_, f32[1024,1536]{1,0:T(8,128)} %get-tuple-element.56.refs_2_, ...), custom_call_target="tpu_custom_call" | custom-call | tf_op jit(solution)/shard_map/pallas_call | solution.py:406
  253.6 7.2 %convolution_convert_fusion.2.refs_4_ = bf16[768,2048]{1,0:T(8,128)(2,1)} fusion(bf16[1024,768]{1,0:T(8,128)(2,1)S(1)} %copy-done.4, bf16[1024,2048]{1,0:T(8,128)(2,1)} %get-tuple-element.67), kind=kOutput, calls=%fused_computation.3 | convolution fusion | flops 3222798336 | bytes 8912896 | tf_op jit(solution)/shard_map/dot_general | solution.py:31
  260.8 8.8 %convolution_convert_fusion.refs_3_ = bf16[2048,1536]{1,0:T(8,128)(2,1)} fusion(bf16[1024,2048]{1,0:T(8,128)(2,1)S(1)} %copy-done.18, bf16[1024,1536]{1,0:T(8,128)(2,1)S(1)} %copy-done.3), kind=kOutput, calls=%fused_computation | convolution fusion | flops 6445596672 | bytes 13631488 | tf_op jit(solution)/shard_map/dot_general | solution.py:31
  269.7 81.8 %shard_map.240 = (bf16[1024,2048]{1,0:T(8,128)(2,1)}, f32[128,2048]{1,0:T(8,128)}, f32[1,2048]{1,0:T(1,128)}, bf16[1024,256]{1,0:T(8,128)(2,1)}, bf16[128,1536]{1,0:T(8,128)(2,1)}, /*index=5*/bf16[768,128]{1,0:T(8,128)(2,1)}) custom-call(bf16[1024,1536]{1,0:T(8,128)(2,1)} %get-tuple-element.65.refs_0_, bf16[2048,1536]{1,0:T(8,128)(2,1)} %get-tuple-element.52.refs_2_.refs_1_, ...), custom_call_target="tpu_custom_call" | custom-call | tf_op jit(solution)/shard_map/pallas_call | solution.py:406
  351.5 3.5 convolution_convert_fusion.3
  355.0 46.6 %shard_map.241 = (bf16[1024,768]{1,0:T(8,128)(2,1)}, f32[2,256]{1,0:T(2,128)}, bf16[1024,1536]{1,0:T(8,128)(2,1)}) custom-call(bf16[1024,256]{1,0:T(8,128)(2,1)} %get-tuple-element.59.refs_0_, bf16[1024,256]{1,0:T(8,128)(2,1)} %get-tuple-element.60.refs_1_, bf16[1024,256]{1,0:T(8,128)(2,1)} %get-tuple-element.61.refs_2_, ...), custom_call_target="tpu_custom_call" | custom-call | tf_op jit(solution)/shard_map/pallas_call | solution.py:406
  404.2 6.4 %convolution_convert_fusion.1.refs_2_ = bf16[2048,768]{1,0:T(8,128)(2,1)} fusion(bf16[1024,2048]{1,0:T(8,128)(2,1)S(1)} %copy-done.17, bf16[1024,768]{1,0:T(8,128)(2,1)} %get-tuple-element.71.refs_0_), kind=kOutput, calls=%fused_computation.2 | convolution fusion | flops 3222798336 | bytes 8912896 | tf_op jit(solution)/shard_map/dot_general | solution.py:31
  410.5 46.7 %shard_map.242 = (f32[128,2048]{1,0:T(8,128)}, bf16[128,768]{1,0:T(8,128)(2,1)}, bf16[288,128]{1,0:T(8,128)(2,1)}) custom-call(bf16[1024,768]{1,0:T(8,128)(2,1)} %get-tuple-element.71.refs_0_, bf16[2048,768]{1,0:T(8,128)(2,1)} %get-tuple-element.72.refs_1_, bf16[2048,768]{1,0:T(8,128)(2,1)} %convolution_convert_fusion.1.refs_2_, ...), custom_call_target="tpu_custom_call" | custom-call | tf_op jit(solution)/shard_map/pallas_call | solution.py:406
  458.1 3.0 collective-permute-start.2
  462.0 1.5 fusion.18
  464.8 1.5 copy.47
  466.3 1.5 convert_element_type.123
  467.9 2.2 copy.45
  470.1 2.5 copy.48
  472.6 1.5 convert_element_type.124
  474.2 2.2 copy.46
  478.1 41.6 %shard_map.243 = (bf16[1024,768]{1,0:T(8,128)(2,1)}, bf16[3840,256]{1,0:T(8,128)(2,1)}, bf16[256,128]{1,0:T(8,128)(2,1)}) custom-call(bf16[128,768]{1,0:T(8,128)(2,1)} %get-tuple-element.80.refs_0_, bf16[480,256]{1,0:T(8,128)(2,1)} %pad_maximum_fusion.1.refs_1_, bf16[32,128]{1,0:T(8,128)(2,1)} %slice.92.refs_2_), custom_call_target="tpu_custom_call" | custom-call | tf_op jit(solution)/shard_map/pallas_call | solution.py:406
  519.7 1.9 convert_bitcast_fusion
  521.9 2.0 copy.53
  (96 shorter events, 24.9 us)
Async XLA Ops:
  0.6 7.3 %copy-start = (bf16[128,2048]{1,0:T(8,128)(2,1)S(1)}, bf16[128,2048]{1,0:T(8,128)(2,1)}, u32[]{:S(2)}) copy-start(bf16[128,2048]{1,0:T(8,128)(2,1)} %param.16) | copy-start | bytes 1572868
  0.7 6.9 %copy-start.12 = (s32[8,2]{0,1:T(2,128)S(1)}, s32[8,2]{0,1:T(2,128)}, u32[]{:S(2)}) copy-start(s32[8,2]{0,1:T(2,128)} %param.27) | copy-start | bytes 196
  1.8 12.1 %copy-start.13 = (bf16[128]{0:T(256)(128)(2,1)S(1)}, bf16[128]{0:T(256)(128)(2,1)}, u32[]{:S(2)}) copy-start(bf16[128]{0:T(256)(128)(2,1)} %param.26) | copy-start | bytes 772
  1.8 12.1 %copy-start.14 = (bf16[128]{0:T(256)(128)(2,1)S(1)}, bf16[128]{0:T(256)(128)(2,1)}, u32[]{:S(2)}) copy-start(bf16[128]{0:T(256)(128)(2,1)} %param.25) | copy-start | bytes 772
  1.9 12.1 %copy-start.15 = (bf16[128]{0:T(256)(128)(2,1)S(1)}, bf16[128]{0:T(256)(128)(2,1)}, u32[]{:S(2)}) copy-start(bf16[128]{0:T(256)(128)(2,1)} %param.24) | copy-start | bytes 772
  1.9 12.1 %copy-start.16 = (bf16[128]{0:T(256)(128)(2,1)S(1)}, bf16[128]{0:T(256)(128)(2,1)}, u32[]{:S(2)}) copy-start(bf16[128]{0:T(256)(128)(2,1)} %param.23) | copy-start | bytes 772
  3.4 13.8 %collective-permute-start = (bf16[480,128]{1,0:T(8,128)(2,1)S(1)}, bf16[480,128]{1,0:T(8,128)(2,1)S(1)}, u32[]{:S(2)}, u32[]{:S(2)}) collective-permute-start(bf16[480,128]{1,0:T(8,128)(2,1)S(1)} %get-tuple-element.102), channel_id=1, source_target_pairs={{0,0},{1,1},{2,16},{3,17},{4,32},{5,33},{6,48},{7,49},{8,64},{9,65... | collective-permute-start | bytes 368648 | tf_op jit(solution)/shard_map/ppermute | solution.py:1190
  7.2 10.0 %collective-permute-start.1 = (bf16[480,128]{1,0:T(8,128)(2,1)S(1)}, bf16[480,128]{1,0:T(8,128)(2,1)S(1)}, u32[]{:S(2)}, u32[]{:S(2)}) collective-permute-start(bf16[480,128]{1,0:T(8,128)(2,1)S(1)} %get-tuple-element.103), channel_id=1, source_target_pairs={{0,1},{1,0},{2,17},{3,16},{4,33},{5,32},{6,49},{7,48},{8,65},{9,64... | collective-permute-start | bytes 368648 | tf_op jit(solution)/shard_map/ppermute | solution.py:1190
  181.3 72.3 %copy-start.4 = (bf16[1024,768]{1,0:T(8,128)(2,1)S(1)}, bf16[1024,768]{1,0:T(8,128)(2,1)}, u32[]{:S(2)}) copy-start(bf16[1024,768]{1,0:T(8,128)(2,1)} %get-tuple-element.54.refs_0_) | copy-start | bytes 4718596
  253.6 7.2 %copy-start.3 = (bf16[1024,1536]{1,0:T(8,128)(2,1)S(1)}, bf16[1024,1536]{1,0:T(8,128)(2,1)}, u32[]{:S(2)}) copy-start(bf16[1024,1536]{1,0:T(8,128)(2,1)} %get-tuple-element.65.refs_0_) | copy-start | bytes 9437188
  253.6 7.2 %copy-start.18 = (bf16[1024,2048]{1,0:T(8,128)(2,1)S(1)}, bf16[1024,2048]{1,0:T(8,128)(2,1)}, u32[]{:S(2)}) copy-start(bf16[1024,2048]{1,0:T(8,128)(2,1)} %get-tuple-element.66) | copy-start | bytes 12582916
  269.7 81.8 %copy-start.7 = (bf16[1024,256]{1,0:T(8,128)(2,1)S(1)}, bf16[1024,256]{1,0:T(8,128)(2,1)}, u32[]{:S(2)}) copy-start(bf16[1024,256]{1,0:T(8,128)(2,1)} %get-tuple-element.50.refs_0_) | copy-start | bytes 1572868
  355.0 48.0 %copy-start.11 = (f32[1,2048]{1,0:T(1,128)S(1)}, f32[1,2048]{1,0:T(1,128)}, u32[]{:S(2)}) copy-start(f32[1,2048]{1,0:T(1,128)} %get-tuple-element.76) | copy-start | bytes 24580
  355.0 48.0 %copy-start.10 = (f32[1,2048]{1,0:T(1,128)S(1)}, f32[1,2048]{1,0:T(1,128)}, u32[]{:S(2)}) copy-start(f32[1,2048]{1,0:T(1,128)} %get-tuple-element.77) | copy-start | bytes 24580
  355.0 49.2 %copy-start.17 = (bf16[1024,2048]{1,0:T(8,128)(2,1)S(1)}, bf16[1024,2048]{1,0:T(8,128)(2,1)}, u32[]{:S(2)}) copy-start(bf16[1024,2048]{1,0:T(8,128)(2,1)} %get-tuple-element.73) | copy-start | bytes 12582916
  410.5 47.5 %copy-start.9 = (bf16[768,128]{1,0:T(8,128)(2,1)S(1)}, bf16[768,128]{1,0:T(8,128)(2,1)}, u32[]{:S(2)}) copy-start(bf16[768,128]{1,0:T(8,128)(2,1)} %get-tuple-element.82) | copy-start | bytes 589828
  410.5 51.5 %copy-start.2 = (bf16[1024,1536]{1,0:T(8,128)(2,1)S(1)}, bf16[1024,1536]{1,0:T(8,128)(2,1)}, u32[]{:S(2)}) copy-start(bf16[1024,1536]{1,0:T(8,128)(2,1)} %get-tuple-element.85) | copy-start | bytes 9437188
  458.1 18.3 %collective-permute-start.2 = (bf16[480,128]{1,0:T(8,128)(2,1)S(1)}, bf16[480,128]{1,0:T(8,128)(2,1)S(1)}, u32[]{:S(2)}, u32[]{:S(2)}) collective-permute-start(bf16[480,128]{1,0:T(8,128)(2,1)S(1)} %get-tuple-element.109), channel_id=1, source_target_pairs={{0,0},{1,1},{16,2},{17,3},{32,4},{33,5},{48,6},{49,7},{64,8},{65,9... | collective-permute-start | bytes 368648 | tf_op jit(solution)/shard_map/ppermute | solution.py:1269
  461.1 15.3 %collective-permute-start.3 = (bf16[480,128]{1,0:T(8,128)(2,1)S(1)}, bf16[480,128]{1,0:T(8,128)(2,1)}, u32[]{:S(2)}, u32[]{:S(2)}) collective-permute-start(bf16[480,128]{1,0:T(8,128)(2,1)S(1)} %get-tuple-element.110), channel_id=1, source_target_pairs={{1,0},{0,1},{17,2},{16,3},{33,4},{32,5},{49,6},{48,7},{65,8},{64,9... | collective-permute-start | bytes 368648 | tf_op jit(solution)/shard_map/ppermute | solution.py:1269
  521.9 3.1 copy-start.5
  525.3 4.5 copy-start.8
  526.4 4.2 copy-start.6
  526.4 5.2 copy-start.1
where the time goes:
time: 541 us; the launch traced here: 532 us
  Pallas kernels  452 us (84%)
  local copies, waits for them, and re-layouts  29.5 us (5%)
  matrix products  25.8 us (5%)
  other arithmetic  15.7 us (3%)
  starting transfers between devices  7.91 us (1%)
    pallas_call x7, Pallas kernels, launch(): pl.pallas_call(kernel, out_shape=[out for out, _ in outs.values()], in_sp...  452 us
    dot_general x4, matrix products, outer_sum(): lax.dot_general(left, right, (((0,), (0,)), ((), ())), preferred_element_...  25.8 us
    unnamed x47, local copies, waits for them, and re-layouts  11.8 us
  transfers between devices with their start and end apart: 4, of which 0 were waited for; matrix products, arithmetic and copies ran while one was open for 5% of the time, Pallas kernels for 0%

commit v1 on v0

--- a/solution.py
+++ b/solution.py
@@ -1,7 +1,9 @@
+import functools
 import types
 
 import jax
 import jax.numpy as jnp
+import numpy as np
 from jax import lax
 from jax.experimental import pallas as pl
 from jax.experimental.pallas import tpu as pltpu
@@ -17,10 +19,10 @@
 NEG = -1e30
 
 
-def angles(positions):
-    freqs = THETA ** (-jnp.arange(0, HD, 2, dtype=F32) / HD)
-    phase = positions.astype(F32)[:, None] * jnp.tile(freqs, 4)[None, :]
-    return jnp.cos(phase), jnp.sin(phase)
+def angles(length):
+    freqs = THETA ** (-np.arange(0, HD, 2, dtype=np.float32) / np.float32(HD))
+    phase = np.arange(length, dtype=np.float32)[:, None] * np.tile(freqs, 4)[None, :]
+    return jnp.asarray(np.cos(phase)), jnp.asarray(np.sin(phase))
 
 
 def dot(left, right):
@@ -136,6 +138,14 @@
         high_row = self.rows if high_row is None else high_row
         start = pl.multiple_of(index * self.rows + low_row, 16)
         return self.ref.at[pl.ds(start, high_row - low_row)]
+
+
+class Chips(Rows):
+    def __init__(self, ref, owners):
+        super().__init__(ref, owners // 2)
+
+    def block(self, index, low_row=0, high_row=None):
+        return super().block(lax.div(index, 2), low_row, high_row)
 
 
 class Strips:
@@ -328,8 +338,7 @@
 def owner_gather(owner, copies, stores, items):
     sibling = {owner.axis: owner.sibling}
     passed, own = [], True
-    for mine, whole in items:
-        stores.start(mine, whole.block(owner.me))
+    placed = [stores.start(mine, whole.block(owner.me)) for mine, whole in items]
     for indexes in ring_gather(owner, copies, items):
         for index in indexes:
             for mine, whole in items:
@@ -338,6 +347,8 @@
         own = False
         yield
     arrived(passed)
+    for copy in placed:
+        copy.wait()
     yield
 
 
@@ -363,6 +374,7 @@
             give.wait_recv()
             add(item.parts.block(owner.at(other, step)), [landed])
 
+    yield
     yield from ring_scatter(owner, copies, sums, prepare)
     for item in sums:
         item.out[...] = low(item.total(owner))
@@ -371,7 +383,7 @@
 
 def sum_scratch(rows, columns, owners):
     return [
-        pltpu.VMEM((owners * rows, columns), BF16),
+        pltpu.VMEM((owners // 2 * rows, columns), BF16),
         pltpu.VMEM((owners // 2, rows, columns), BF16),
         *landing(rows, columns),
     ]
@@ -424,14 +436,19 @@
     return {name: (array, FAR) for name, array in arrays.items()}
 
 
-def tiles(product, rows, value, weight, tile, transposed):
+def tiles(product, rows, values, weight, tile, transposed):
+    size = values[0].shape[0]
+    value = values[0] if len(values) == 1 else jnp.concatenate(values, axis=0)
+
     def step(i, carry):
         span = rows_at(i, tile)
         if transposed:
             piece = back_dot(value, weight[span, :])
         else:
             piece = dot(value, weight[:, span])
-        product[rows, span] = piece.astype(product.dtype)
+        piece = piece.astype(product.dtype)
+        for k, at in enumerate(rows):
+            product[at, span] = piece[k * size : (k + 1) * size]
         return carry
 
     lax.fori_loop(0, product.shape[1] // tile, step, 0)
@@ -459,36 +476,35 @@
         self.ready += [(self.fresh, index) for index in next(self.stream)]
         self.fresh = False
 
-    def consume(self):
-        for own, index in self.ready:
-            src = self.block if own else self.landed.block(index)
-            self.stores.start(src, self.whole.block(index))
-            self.use(src, index)
-        self.ready = []
-
-
-def gathered_all(gathered, pump):
+    def consume(self, last=True):
+        while len(self.ready) > (0 if last else 1):
+            pair, self.ready = self.ready[:2], self.ready[2:]
+            sources = [self.block if own else self.landed.block(index) for own, index in pair]
+            for src, (_, index) in zip(sources, pair):
+                self.stores.start(src, self.whole.block(index))
+            self.use(sources, [rows_at(index, self.landed.rows) for _, index in pair])
+
+
+def gathered_all(gathered):
+    for _ in range(4):
+        gathered.consume(False)
+        gathered.step()
     gathered.consume()
-    for _ in range(4):
-        pump()
-        gathered.step()
-        gathered.consume()
-
-
-def ctx_sum(group, copies, act, weight, item, tile, transposed):
-    parts = item.parts
+
+
+def ctx_sum(group, copies, act, weight, items, tile, transposed):
+    parts = items[0].parts
 
     def prepare(other, step):
         rows = rows_at(group.at(other, step), parts.rows)
-        tiles(parts.ref, rows, act[rows, :], weight, tile, transposed)
-
-    return ring_scatter(group, copies, [item], prepare, True)
+        tiles(parts.ref, [rows], [act[rows, :]], weight, tile, transposed)
+
+    return ring_scatter(group, copies, items, prepare, True)
 
 
 def weave(main, stream):
-    for _ in main:
-        if stream is not None:
-            next(stream, None)
+    for step in "000110101010101":
+        next(stream if step == "1" else main)
 
 
 def finish(stream):
@@ -504,10 +520,6 @@
 def norm_back(grad, unit, inverse, gain):
     pull = grad * gain
     return inverse * (pull - unit * jnp.mean(pull * unit, axis=-1, keepdims=True))
-
-
-def head_lanes(shape):
-    return lax.broadcasted_iota(jnp.int32, shape, 1) < HD
 
 
 def turn_lanes(shape):
@@ -528,15 +540,8 @@
     return jnp.where(turn_lanes(values.shape), ahead, -behind)
 
 
-def soft(keys, query, key_pos, query_pos):
-    scores = back_dot(keys, query) * HD ** (-0.5)
-    scores = jnp.where(query_pos >= key_pos, scores, NEG)
-    expo = jnp.exp(scores - jnp.max(scores, axis=0, keepdims=True))
-    return expo / jnp.sum(expo, axis=0, keepdims=True)
-
-
 def heads_of(query):
-    first = head_lanes(query.shape)
+    first = lax.broadcasted_iota(jnp.int32, query.shape, 1) < HD
     return first, jnp.logical_not(first)
 
 
@@ -544,7 +549,42 @@
     return jnp.concatenate([outs[0][:HD], outs[1][HD:]], axis=0)
 
 
-def attend(block, qkv_mine, gains_mine, out_mine, gate_up_mine, cosine, sine, positions, number):
+def soft(keys, span, query, start):
+    chunk = query.shape[0]
+    own = back_dot(keys[pl.ds(start, chunk), span], query)
+    behind = lax.broadcasted_iota(jnp.int32, own.shape, 0) <= lax.broadcasted_iota(
+        jnp.int32, own.shape, 1
+    )
+    pieces = [jnp.where(behind, own, NEG)]
+    if start:
+        pieces.insert(0, back_dot(keys[pl.ds(0, start), span], query))
+    top = jnp.max(pieces[-1], axis=0, keepdims=True)
+    for piece in pieces[:-1]:
+        top = jnp.maximum(top, jnp.max(piece, axis=0, keepdims=True))
+    pieces = [jnp.exp(piece - top) for piece in pieces]
+    total = sum(jnp.sum(piece, axis=0, keepdims=True) for piece in pieces)
+    places = [pl.ds(0, start), pl.ds(start, chunk)][-len(pieces) :]
+    return list(zip(places, pieces)), 1.0 / total
+
+
+def placing(query_pos):
+    length = query_pos.shape[1]
+    row = lax.broadcasted_iota(jnp.int32, (length, length), 0)
+    return low(jnp.where(row == query_pos[...], 1.0, 0.0))
+
+
+def dealing(key_pos):
+    length = key_pos.shape[0]
+    column = lax.broadcasted_iota(jnp.int32, (length, length), 1)
+    return low(jnp.where(column == key_pos[...], 1.0, 0.0))
+
+
+def split(values):
+    high = low(values)
+    return high, low(values - high.astype(F32))
+
+
+def attend(block, qkv_mine, gains_mine, out_mine, gate_mine, cosine, sine, orders, number):
     ranks, owners = lax.axis_size("ctx"), lax.axis_size("fsdp")
     (size, depth), columns = block.shape, qkv_mine.shape[1]
     length, share, chunk = ranks * size, columns // 3, 256
@@ -552,18 +592,18 @@
 
     def body(r, copies, stores):
         group, owner = Group("ctx"), Group("fsdp")
-        others = [{"ctx": lax.rem(group.me + step, ranks)} for step in range(1, ranks)]
-        meet(others + owner.peers())
+        others = [lax.rem(group.me + step, ranks) for step in (2, 6, 4, 1, 3, 5, 7)]
+        meet([{"ctx": other} for other in others] + owner.peers())
         normed = 2 * share
         by_lane = lax.broadcasted_iota(jnp.int32, (8, normed), 1) < share
         by_row = lax.broadcasted_iota(jnp.int32, (8, normed), 0) < 4
         select = jnp.where(by_lane == by_row, 1.0, 0.0)
 
-        def use(src, index):
-            rows = rows_at(index, size)
-            tiles(r.proj, rows, src[...], r.qkv_near, 256, False)
-            value = r.proj[rows, pl.ds(0, normed)]
-            r.sums[:, rows] = totals_by_row(select, value * value)
+        def use(sources, places):
+            tiles(r.proj, places, [src[...] for src in sources], r.qkv_near, columns, False)
+            for rows in places:
+                value = r.proj[rows, pl.ds(0, normed)]
+                r.sums[:, rows] = totals_by_row(select, value * value)
 
         gathered = Gathered(group, copies, stores, r.block, r.landed, r.whole, use)
         gains_all = Rows(r.gains_near, owners)
@@ -573,15 +613,9 @@
             stores,
             [(r.qkv_mine, Rows(r.qkv_near, owners)), (r.gains_mine, gains_all)],
         )
-        second = owner_gather(
-            owner,
-            copies,
-            stores,
-            [
-                (r.out_mine, Strips(r.out_near, owners)),
-                (r.gate_up_mine, Rows(r.gate_up_near, owners)),
-            ],
-        )
+        second = owner_gather(owner, copies, stores, [(r.out_mine, Rows(r.out_near, owners))])
+        third = owner_gather(owner, copies, stores, [(r.gate_mine, Rows(r.gate_near, owners))])
+
         next(first)
         gathered.step()
         next(first)
@@ -590,56 +624,90 @@
         next(second)
         gathered.step()
         finish(first)
+        gathered.step()
         stores.drain()
         stores.start(r.qkv_near, r.qkv)
+        gathered.consume(False)
+        next(second)
+        gathered.step()
+        gathered.consume(False)
+        gathered.step()
         gathered.consume()
-        for _ in range(3):
-            next(second)
-            gathered.step()
-            gathered.consume()
-        exchange = [copies.start(r.sums, r.sums_landed.at[i], to) for i, to in enumerate(others)]
+        exchange = [
+            copies.start(r.sums, r.sums_landed.at[i], {"ctx": other})
+            for i, other in enumerate(others)
+        ]
+        next(second)
         for i in range(owners):
             rows = r.gains_near[pl.ds(i * gains_all.rows, 16), :].astype(F32)
             r.scales[:, pl.ds(i * rows.shape[1], rows.shape[1])] = rows[:8]
+        next(second)
+        next(third)
         arrived(exchange)
         totals = r.sums[...] + jnp.sum(r.sums_landed[...], axis=0)
-        r.inverse[...] = lax.rsqrt(totals * (1.0 / (ranks * share)) + EPSILON).T
+        r.inverse_dealt[...] = lax.rsqrt(totals * (1.0 / (ranks * share)) + EPSILON).T
         mine = rows_at(group.me, share)
-        for i, (unit, out) in enumerate(((r.query_unit, r.queries), (r.key_unit, r.keys))):
-            span = pl.ds(i * share, share)
-            unit[...] = r.proj[:, span] * r.inverse[:, 4 * i : 4 * i + 1]
-            gain = r.scales[i : i + 1, mine]
+
+        wide = r.stack.shape[1] - share
+        for k in range(2):
+            span = pl.ds(k * share, share)
+            unit = r.proj[:, span] * r.inverse_dealt[:, 4 * k : 4 * k + 1]
+            for half, part in enumerate(split(unit)):
+                r.stack[:, pl.ds((2 * k + half) * share, share)] = part
+        r.stack[:, pl.ds(wide, share)] = low(r.proj[:, pl.ds(2 * share, share)])
+        order = placing(r.query_pos)
+        high, rest = split(r.inverse_dealt[...])
+        r.inverse[...] = dot(order, high) + dot(order, rest)
+        for k, (unit, out) in enumerate(((r.query_unit, r.queries), (r.key_unit, r.keys))):
+            both = dot(order, r.stack[:, pl.ds(2 * k * share, 2 * share)])
+            unit[...] = both[:, :share] + both[:, share:]
+            scaled = unit[...] * r.scales[k : k + 1, mine]
             for pair in range(share // lanes):
-                part = pl.ds(pair * lanes, lanes)
-                scaled = unit[:, part] * gain[:, pair * lanes : (pair + 1) * lanes]
-                out[:, part] = low(scaled * r.cosine[...] + turned(scaled) * r.sine[...])
-        r.values[...] = low(r.proj[:, pl.ds(2 * share, share)])
-
+                part = scaled[:, pair * lanes : (pair + 1) * lanes]
+                out[:, pl.ds(pair * lanes, lanes)] = low(
+                    part * r.cosine[...] + turned(part) * r.sine[...]
+                )
+        r.values[...] = low(dot(order, r.stack[:, pl.ds(wide, share)]))
+        r.deal[...] = dealing(r.key_pos)
+        crossing = []
         for pair in range(share // lanes):
             span = pl.ds(pair * lanes, lanes)
             value_turned = r.values[:, span].astype(F32).T.astype(BF16)
-
-            def step(i, carry):
-                rows = rows_at(i, chunk)
-                query = r.queries[rows, span]
+            for start in range(0, length, chunk):
+                rows = pl.ds(start, chunk)
+                query = r.queries[rows, span] * BF16(HD ** (-0.5))
                 nothing = jnp.zeros_like(query)
                 outs = []
                 for mask in heads_of(query):
-                    query_head = jnp.where(mask, query, nothing)
-                    probs = soft(r.keys[:, span], query_head, r.key_pos[...], r.query_pos[:, rows])
-                    outs.append(dot(value_turned, low(probs)))
-                r.mixed[rows, span] = low(pair_of(outs).T)
-                return carry
-
-            steps = length // chunk
-            lax.fori_loop(0, steps // 2, step, 0)
-            next(second, None)
-            lax.fori_loop(steps // 2, steps, step, 0)
-            next(second, None)
+                    pieces, over = soft(r.keys, span, jnp.where(mask, query, nothing), start)
+                    out = sum(
+                        dot(value_turned[:, at.start : at.start + at.size], low(piece))
+                        for at, piece in pieces
+                    )
+                    outs.append(out * over)
+                r.mixed[rows, :] = low(pair_of(outs).T)
+                if start == length // 2:
+                    next(second if pair == 0 else third)
+
+            r.mixed_dealt[:, span] = low(dot(r.deal[...], r.mixed[...]))
+            at = pl.ds(pl.multiple_of(group.me * share + pair * lanes, lanes), lanes)
+            for other in others:
+                src = r.mixed_dealt.at[rows_at(other, size), span]
+                crossing.append(copies.start(src, r.mixed_landed.at[:, at], {"ctx": other}))
+            r.mixed_landed[:, at] = r.mixed_dealt[rows_at(group.me, size), span]
+            next(third)
         finish(second)
+        arrived(crossing)
         stores.drain()
-        stores.start(r.out_near, r.out_rows)
-        stores.start(r.gate_up_near, r.gate_up)
+        stores.start(r.out_near, r.out_whole)
+        r.mixed_rows[...] = r.mixed_landed[...]
+        tiles(r.attn_raw, [pl.ds(0, size)], [r.mixed_landed[...]], r.out_near, 512, False)
+        unit, _ = norm(r.attn_raw[...])
+        hidden = r.block[...].astype(F32) + unit * r.scales[2:3, :]
+        r.hidden[...] = hidden
+        r.hidden_low[...] = low(hidden)
+        finish(third)
+        stores.start(r.gate_near, r.gate)
         stores.drain()
         copies.drain()
 
@@ -651,17 +719,16 @@
             qkv_mine=qkv_mine,
             gains_mine=gains_mine,
             out_mine=out_mine,
-            gate_up_mine=gate_up_mine,
+            gate_mine=gate_mine,
             cosine=cosine,
             sine=sine,
-            key_pos=positions[:, None],
-            query_pos=positions[None, :],
-        ),
+        )
+        | near(**orders),
         far(
             whole=shape((length, depth)),
             qkv=shape((depth, columns)),
-            out_rows=shape((share, depth)),
-            gate_up=shape((depth, gate_up_mine.shape[1])),
+            out_whole=shape((depth, depth)),
+            gate=shape((depth, gate_mine.shape[1])),
         )
         | near(
             scales=shape((8, depth), F32),
@@ -671,309 +738,282 @@
             queries=shape((length, share)),
             keys=shape((length, share)),
             values=shape((length, share)),
-            mixed=shape((length, share)),
+            mixed_rows=shape((size, depth)),
+            attn_raw=shape((size, depth), F32),
+            hidden=shape((size, depth), F32),
+            hidden_low=shape((size, depth)),
         ),
         dict(
             landed=pltpu.VMEM((length, depth), BF16),
             qkv_near=pltpu.VMEM((depth, columns), BF16),
             gains_near=pltpu.VMEM((owners * gains_mine.shape[0], gains_mine.shape[1]), BF16),
-            out_near=pltpu.VMEM((share, depth), BF16),
-            gate_up_near=pltpu.VMEM((depth, gate_up_mine.shape[1]), BF16),
+            out_near=pltpu.VMEM((depth, depth), BF16),
+            gate_near=pltpu.VMEM((depth, gate_mine.shape[1]), BF16),
             proj=pltpu.VMEM((length, columns), F32),
             sums=pltpu.VMEM((8, length), F32),
             sums_landed=pltpu.VMEM((ranks - 1, 8, length), F32),
+            inverse_dealt=pltpu.VMEM((length, 8), F32),
+            stack=pltpu.VMEM((length, 5 * share), BF16),
+            deal=pltpu.VMEM((length, length), BF16),
+            mixed=pltpu.VMEM((length, lanes), BF16),
+            mixed_dealt=pltpu.VMEM((length, share), BF16),
+            mixed_landed=pltpu.VMEM((size, depth), BF16),
         ),
-        15 + 34 + 34 + ranks - 1,
-        20,
-    )
-
-
-def feed_in(mixed, out_rows, block, scales, gate_up, down_mine, number):
+        15 + 34 + 17 + 17 + 3 * (ranks - 1),
+        24,
+    )
+
+
+def feed(hidden, hidden_low, gate, up_mine, down_mine, cotangent, scales, number):
     ranks, owners = lax.axis_size("ctx"), lax.axis_size("fsdp")
-    size, width = block.shape
-    length, both = mixed.shape[0], gate_up.shape[1]
-    room = both // 2
+    size, width = hidden.shape
+    length, room = ranks * size, gate.shape[1]
+    both = 2 * room
 
     def body(r, copies, stores):
         group, owner = Group("ctx"), Group("fsdp")
-        fetches = [
-            stores.start(r.mixed, r.act),
-            stores.start(r.out_rows, r.out_near),
-            stores.start(r.gate_up, r.gate_up_near),
-        ]
+        gate_fetch = stores.start(r.gate, r.gate_near)
         meet(group.peers() + owner.peers())
-        item = Sum(Rows(r.part, ranks), *r.landings)
-        fetches[0].wait()
-        fetches[1].wait()
-        summed = ctx_sum(group, copies, r.act, r.out_near, item, 512, False)
+        first, second = pl.ds(0, room), pl.ds(room, room)
+
+        def forward(sources, places):
+            values = [src[...] for src in sources]
+            tiles(r.pre.at[:, first], places, values, r.gate_near, room, False)
+            tiles(r.pre.at[:, second], places, values, r.up_near, room, False)
+            for rows in places:
+                gate, up = r.pre[rows, first], r.pre[rows, second]
+                r.product[rows, :] = low(gate * jax.nn.sigmoid(gate) * up)
+
+        gathered = Gathered(group, copies, stores, r.hidden_low, r.landed, r.whole_hidden, forward)
+        up = owner_gather(owner, copies, stores, [(r.up_mine, Rows(r.up_near, owners))])
         down = owner_gather(
             owner, copies, stores, [(r.down_mine, Strips(r.down_near, owners))]
         )
-        next(summed)
-        weave(summed, down)
-        attn_raw = item.total(group)
-        r.attn_raw[...] = attn_raw
-        unit, _ = norm(attn_raw)
-        hidden = r.block[...].astype(F32) + unit * r.scales[2:3, :]
-        r.hidden[...] = hidden
-        r.hidden_low[...] = low(hidden)
-        fetches[2].wait()
-
-        def use(src, index):
-            rows = rows_at(index, size)
-            tiles(r.pre_near, rows, src[...], r.gate_up_near, 512, False)
-            stores.start(r.pre_near.at[rows], r.pre.at[rows])
-            gate, up = r.pre_near[rows, pl.ds(0, room)], r.pre_near[rows, pl.ds(room, room)]
-            r.product[rows, :] = low(gate * jax.nn.sigmoid(gate) * up)
-
-        gathered = Gathered(group, copies, stores, r.hidden_low, r.landed, r.whole, use)
+        next(up)
         gathered.step()
-        gathered_all(gathered, lambda: next(down, None))
+        next(up)
+        next(up)
+        gathered.step()
+        next(up)
+        next(down)
+        gathered.step()
+        finish(up)
+        gate_fetch.wait()
+        gathered.step()
+        next(down)
+        gathered.consume(False)
+        next(down)
+        gathered.step()
+        next(down)
+        gathered.consume()
         finish(down)
         stores.drain()
-        stores.start(r.down_near, r.down_rows).wait()
-        copies.drain()
-
-    return launch(
-        number,
-        body,
-        far(mixed=mixed, out_rows=out_rows, gate_up=gate_up)
-        | near(block=block, scales=scales, down_mine=down_mine),
-        far(
-            whole=shape((length, width)),
-            pre=shape((length, both), F32),
-            down_rows=shape((room, width)),
-        )
-        | near(
-            attn_raw=shape((size, width), F32),
-            hidden=shape((size, width), F32),
-            product=shape((length, room)),
-        ),
-        dict(
-            act=pltpu.VMEM(mixed.shape, BF16),
-            out_near=pltpu.VMEM(out_rows.shape, BF16),
-            gate_up_near=pltpu.VMEM(gate_up.shape, BF16),
-            down_near=pltpu.VMEM((room, width), BF16),
-            part=pltpu.VMEM((length, width), BF16),
-            landings=landing(size, width, True),
-            landed=pltpu.VMEM((length, width), BF16),
-            hidden_low=pltpu.VMEM((size, width), BF16),
-            pre_near=pltpu.VMEM((length, both), F32),
-        ),
-        17 + 15 + 17,
-        22,
-    )
-
-
-def feed_out(product, down_rows, pre, hidden, cotangent, scales, number):
-    ranks = lax.axis_size("ctx")
-    size, width = hidden.shape
-    length, both = pre.shape
-    room = both // 2
-
-    def body(r, copies, stores):
-        group = Group("ctx")
-        fetches = [
-            stores.start(r.product, r.act),
-            stores.start(r.down_rows, r.down_near),
-            stores.start(r.pre, r.pre_near),
-        ]
-        meet(group.peers())
+        stores.start(r.up_near, r.up)
+        stores.start(r.down_near, r.down_rows)
         item = Sum(Rows(r.part, ranks), *r.landings)
-        fetches[0].wait()
-        fetches[1].wait()
-        finish(ctx_sum(group, copies, r.act, r.down_near, item, 512, False))
+        finish(ctx_sum(group, copies, r.product, r.down_near, [item], 512, False))
         unit, inverse = norm(item.total(group))
         gain = r.scales[3:4, :]
         r.result[...] = low(r.hidden[...] + unit * gain)
         upstream = r.cotangent[...].astype(F32)
         r.feed_term[...] = jnp.sum(upstream * unit, axis=0, keepdims=True)
         r.down_low[...] = low(norm_back(upstream, unit, inverse, gain))
-        fetches[2].wait()
-
-        def use(src, index):
-            rows = rows_at(index, size)
-            tiles(r.product_grad, pl.ds(0, size), src[...], r.down_near, 256, True)
-            gate, up = r.pre_near[rows, pl.ds(0, room)], r.pre_near[rows, pl.ds(room, room)]
-            grad, sigmoid = r.product_grad[...], jax.nn.sigmoid(gate)
-            r.both_low[rows, pl.ds(0, room)] = low(
-                grad * up * sigmoid * (1.0 + gate * (1.0 - sigmoid))
-            )
-            r.both_low[rows, pl.ds(room, room)] = low(grad * gate * sigmoid)
-
-        gathered = Gathered(group, copies, stores, r.down_low, r.landed, r.whole, use)
+
+        def backward(sources, places):
+            values = [src[...] for src in sources]
+            tiles(r.product_grad, places, values, r.down_near, room, True)
+            for rows in places:
+                gate, up = r.pre[rows, first], r.pre[rows, second]
+                grad, sigmoid = r.product_grad[rows, :], jax.nn.sigmoid(gate)
+                r.both_low[rows, first] = low(
+                    grad * up * sigmoid * (1.0 + gate * (1.0 - sigmoid))
+                )
+                r.both_low[rows, second] = low(grad * gate * sigmoid)
+
+        gathered = Gathered(group, copies, stores, r.down_low, r.landed_down, r.whole_down, backward)
         gathered.step()
-        gathered_all(gathered, lambda: None)
+        gathered_all(gathered)
         stores.drain()
         copies.drain()
 
     return launch(
         number,
         body,
-        far(product=product, down_rows=down_rows, pre=pre)
-        | near(hidden=hidden, cotangent=cotangent, scales=scales),
-        far(whole=shape((length, width)))
+        far(gate=gate)
+        | near(
+            hidden=hidden,
+            hidden_low=hidden_low,
+            up_mine=up_mine,
+            down_mine=down_mine,
+            cotangent=cotangent,
+            scales=scales,
+        ),
+        far(
+            whole_hidden=shape((length, width)),
+            whole_down=shape((length, width)),
+            up=shape((width, room)),
+            down_rows=shape((room, width)),
+        )
         | near(
             result=shape((size, width)),
             feed_term=shape((1, width), F32),
+            product=shape((length, room)),
             both_low=shape((length, both)),
         ),
         dict(
-            act=pltpu.VMEM(product.shape, BF16),
-            down_near=pltpu.VMEM(down_rows.shape, BF16),
-            pre_near=pltpu.VMEM((length, both), F32),
+            gate_near=pltpu.VMEM((width, room), BF16),
+            up_near=pltpu.VMEM((width, room), BF16),
+            down_near=pltpu.VMEM((room, width), BF16),
+            landed=pltpu.VMEM((length, width), BF16),
+            pre=pltpu.VMEM((length, both), F32),
             part=pltpu.VMEM((length, width), BF16),
             landings=landing(size, width, True),
-            landed=pltpu.VMEM((length, width), BF16),
+            landed_down=pltpu.VMEM((length, width), BF16),
             down_low=pltpu.VMEM((size, width), BF16),
-            product_grad=pltpu.VMEM((size, room), F32),
+            product_grad=pltpu.VMEM((length, room), F32),
         ),
-        17 + 15,
-        12,
-    )
-
-
-def hidden_back(
-    both_low, gate_up, cotangent, attn_raw, scales, out_rows, gate_up_grad, down_grad, number
-):
+        15 + 15 + 17 + 34,
+        24,
+    )
+
+
+def hidden_back(both_low, gate, up, cotangent, attn_raw, scales, out_whole, gate_up_grad, number):
     ranks, owners = lax.axis_size("ctx"), lax.axis_size("fsdp")
     size, width = attn_raw.shape
     length, both = both_low.shape
-    share = out_rows.shape[0]
+    room, share = both // 2, width // ranks
     gate_up_block = (gate_up_grad.shape[0] // owners, both)
-    down_block = (down_grad.shape[0], width // owners)
 
     def body(r, copies, stores):
         group, owner = Group("ctx"), Group("fsdp")
+        others = [lax.rem(group.me + step, ranks) for step in (2, 6, 4, 1, 3, 5, 7)]
         fetches = [
             stores.start(r.both_low, r.act),
-            stores.start(r.gate_up, r.gate_up_near),
-            stores.start(r.out_rows, r.out_near),
+            stores.start(r.gate, r.gate_up_near.at[:, pl.ds(0, room)]),
+            stores.start(r.up, r.gate_up_near.at[:, pl.ds(room, room)]),
         ]
-        meet(group.peers() + owner.peers())
+        out_fetch = stores.start(r.out_whole, r.out_near)
+        meet([{"ctx": other} for other in others] + owner.peers())
         item = Sum(Rows(r.part, ranks), *r.landings)
-        owned = []
-        for grad, out, scratch in (
-            (Rows(r.gate_up_grad, owners), r.gate_up_share, r.gate_up_sum),
-            (Strips(r.down_grad, owners), r.down_share, r.down_sum),
-        ):
-            part, from_sibling, *places = scratch
-            own = Sum(Rows(part, owners), *places, out)
-            owned.append(owner_sum(owner, copies, stores, [grad], [own], [from_sibling]))
-        next(owned[0])
-        fetches[0].wait()
-        fetches[1].wait()
-        weave(ctx_sum(group, copies, r.act, r.gate_up_near, item, 512, True), owned[0])
+        part, from_sibling, *places = r.gate_up_sum
+        own = Sum(Chips(part, owners), *places, r.gate_up_share)
+        owned = owner_sum(
+            owner, copies, stores, [Rows(r.gate_up_grad, owners)], [own], [from_sibling]
+        )
+        for fetch in fetches:
+            fetch.wait()
+        next(owned)
+        weave(ctx_sum(group, copies, r.act, r.gate_up_near, [item], 512, True), owned)
         hidden_grad = r.cotangent[...].astype(F32) + item.total(group)
         r.hidden_grad[...] = hidden_grad
         unit, inverse = norm(r.attn_raw[...])
         r.attn_term[...] = jnp.sum(hidden_grad * unit, axis=0, keepdims=True)
         r.attn_low[...] = low(norm_back(hidden_grad, unit, inverse, r.scales[2:3, :]))
-        fetches[2].wait()
-
-        def use(src, index):
-            tiles(r.mixed_grad, rows_at(index, size), src[...], r.out_near, 256, True)
-
-        gathered = Gathered(group, copies, stores, r.attn_low, r.landed, r.whole, use)
-        gathered.step()
-        finish(owned[0])
-
-        def pump():
-            next(owned[1], None)
-            next(owned[1], None)
-
-        gathered_all(gathered, pump)
-        finish(owned[1])
+        out_fetch.wait()
+        value = r.attn_low[...]
+        mine = rows_at(group.me, size)
+        crossing = []
+        for i, other in enumerate(others):
+            r.mixed_out[i] = low(back_dot(value, r.out_near[rows_at(other, share), :]))
+            crossing.append(
+                copies.start(r.mixed_out.at[i], r.mixed_landed.at[mine], {"ctx": other})
+            )
+        r.mixed_landed[mine, :] = low(back_dot(value, r.out_near[rows_at(group.me, share), :]))
+        finish(owned)
+        arrived(crossing)
+        r.mixed_grad[...] = r.mixed_landed[...]
         stores.drain()
         copies.drain()
 
     return launch(
         number,
         body,
-        far(
-            both_low=both_low,
-            gate_up=gate_up,
-            out_rows=out_rows,
-            gate_up_grad=gate_up_grad,
-            down_grad=down_grad,
-        )
+        far(both_low=both_low, gate=gate, up=up, out_whole=out_whole, gate_up_grad=gate_up_grad)
         | near(cotangent=cotangent, attn_raw=attn_raw, scales=scales),
-        far(whole=shape((length, width)))
-        | near(
+        near(
             hidden_grad=shape((size, width), F32),
             attn_term=shape((1, width), F32),
+            attn_low=shape((size, width)),
             mixed_grad=shape((length, share)),
             gate_up_share=shape(gate_up_block),
-            down_share=shape(down_block),
         ),
         dict(
             act=pltpu.VMEM(both_low.shape, BF16),
-            gate_up_near=pltpu.VMEM(gate_up.shape, BF16),
-            out_near=pltpu.VMEM(out_rows.shape, BF16),
+            gate_up_near=pltpu.VMEM((width, both), BF16),
+            out_near=pltpu.VMEM(out_whole.shape, BF16),
             part=pltpu.VMEM((length, width), BF16),
             landings=landing(size, width, True),
-            landed=pltpu.VMEM((length, width), BF16),
-            attn_low=pltpu.VMEM((size, width), BF16),
+            mixed_out=pltpu.VMEM((ranks - 1, size, share), BF16),
+            mixed_landed=pltpu.VMEM((length, share), BF16),
             gate_up_sum=sum_scratch(*gate_up_block, owners),
-            down_sum=sum_scratch(*down_block, owners),
         ),
-        17 + 15 + 17 + 17,
-        3 + 8 + 8 + 8,
-    )
-
-
-def attend_back(front, mixed_grad, cosine, sine, positions, gate_up_share, number):
-    ranks = lax.axis_size("ctx")
+        17 + 17 + ranks - 1,
+        4 + 8,
+    )
+
+
+def attend_back(front, mixed_grad, cosine, sine, orders, gate_up_share, out_grad, number):
+    ranks, owners = lax.axis_size("ctx"), lax.axis_size("fsdp")
     length, share = mixed_grad.shape
     lanes, chunk = 2 * HD, 256
     whole = (ranks * gate_up_share.shape[0], gate_up_share.shape[1])
+    out_block = (out_grad.shape[0] // owners, out_grad.shape[1])
 
     def body(r, copies, stores):
-        group = Group("ctx")
+        group, owner = Group("ctx"), Group("fsdp")
         others = [{"ctx": lax.rem(group.me + step, ranks)} for step in range(1, ranks)]
-        meet(others)
+        meet(others + owner.peers())
         all_shares, stored = Rows(r.landed, ranks), Rows(r.whole, ranks)
         stream = ring_gather(group, copies, [(r.block, all_shares)], True)
         next(stream)
         stores.start(r.block, stored.block(group.me))
+        part, from_sibling, *places = r.out_sum
+        own = Sum(Chips(part, owners), *places, r.out_share)
+        owned = owner_sum(owner, copies, stores, [Rows(r.out_grad, owners)], [own], [from_sibling])
+        next(owned)
+        next(owned)
         r.key_turn[...] = jnp.zeros_like(r.key_turn)
         r.value_sum[...] = jnp.zeros_like(r.value_sum)
+
+        r.grads[...] = low(dot(placing(r.query_pos), r.mixed_grad[...]))
 
         def advance():
             for index in next(stream, []):
                 stores.start(all_shares.block(index), stored.block(index))
+            next(owned, None)
 
         for pair in range(share // lanes):
             span = pl.ds(pair * lanes, lanes)
             key_turned = r.keys[:, span].astype(F32).T.astype(BF16)
-
-            def step(i, carry):
-                rows = rows_at(i, chunk)
-                query, grad = r.queries[rows, span], r.mixed_grad[rows, span]
+            for start in range(0, length, chunk):
+                rows = pl.ds(start, chunk)
+                query, grad = r.queries[rows, span] * BF16(HD ** (-0.5)), r.grads[rows, span]
                 nothing = jnp.zeros_like(query)
                 outs = []
                 for mask in heads_of(query):
                     query_head = jnp.where(mask, query, nothing)
                     grad_head = jnp.where(mask, grad, nothing)
-                    probs = soft(r.keys[:, span], query_head, r.key_pos[...], r.query_pos[:, rows])
-                    prob_grad = back_dot(r.values[:, span], grad_head)
-                    delta = jnp.sum(probs * prob_grad, axis=0, keepdims=True)
-                    score_low = low(probs * (prob_grad - delta))
-                    r.value_sum[:, span] += dot(low(probs), grad_head)
-                    r.key_turn[:, span] += dot(score_low, query_head)
-                    outs.append(dot(key_turned, score_low))
+                    pieces, over = soft(r.keys, span, query_head, start)
+                    probs = [piece * over for _, piece in pieces]
+                    prob_grads = [back_dot(r.values[at, span], grad_head) for at, _ in pieces]
+                    delta = sum(
+                        jnp.sum(prob * prob_grad, axis=0, keepdims=True)
+                        for prob, prob_grad in zip(probs, prob_grads)
+                    )
+                    out = 0.0
+                    for (at, _), prob, prob_grad in zip(pieces, probs, prob_grads):
+                        score_low = low(prob * (prob_grad - delta))
+                        r.value_sum[at, span] += dot(low(prob), grad_head)
+                        r.key_turn[at, span] += dot(score_low, query_head)
+                        out += dot(key_turned[:, at.start : at.start + at.size], score_low)
+                    outs.append(out)
                 query_rot = (pair_of(outs) * HD ** (-0.5)).T
                 r.query_turn[rows, span] = query_rot * r.cosine[rows, :] + turned_back(
                     query_rot * r.sine[rows, :]
                 )
-                return carry
-
-            steps = length // chunk
-            lax.fori_loop(0, steps // 2, step, 0)
-            advance()
-            lax.fori_loop(steps // 2, steps, step, 0)
-            advance()
-            key_rot = r.key_turn[:, span] * HD ** (-0.5)
+                if start % (2 * chunk):
+                    advance()
+            key_rot = r.key_turn[:, span]
             r.key_turn[:, span] = key_rot * r.cosine[...] + turned_back(key_rot * r.sine[...])
         by_row = lax.broadcasted_iota(jnp.int32, (8, share), 0) < 4
         mine = rows_at(group.me, share)
@@ -987,6 +1027,7 @@
             )
             r.sums[...] = part if i == 0 else r.sums[...] + part
         exchange = [copies.start(r.sums, r.sums_landed.at[i], to) for i, to in enumerate(others)]
+        advance()
         arrived(exchange)
         totals = r.sums[...] + jnp.sum(r.sums_landed[...], axis=0)
         means = (totals * (1.0 / (ranks * share))).T
@@ -994,12 +1035,14 @@
             ((r.query_turn, r.query_unit), (r.key_turn, r.key_unit))
         ):
             column = slice(4 * i, 4 * i + 1)
-            r.qkv_low[:, pl.ds(i * share, share)] = low(
+            r.placed_low[:, pl.ds(i * share, share)] = low(
                 r.inverse[:, column]
                 * (turn[...] * r.scales[i : i + 1, mine] - unit[...] * means[:, column])
             )
-        r.qkv_low[:, pl.ds(2 * share, share)] = low(r.value_sum[...])
-        for _ in range(5):
+        r.placed_low[:, pl.ds(2 * share, share)] = low(r.value_sum[...])
+
+        r.qkv_low[...] = low(dot(dealing(r.key_pos), r.placed_low[...]))
+        for _ in range(10):
             advance()
         copies.drain()
         stores.drain()
@@ -1018,64 +1061,81 @@
             mixed_grad=mixed_grad,
             cosine=cosine,
             sine=sine,
-            key_pos=positions[:, None],
-            query_pos=positions[None, :],
             block=gate_up_share,
-        ),
-        near(qkv_low=shape((length, 3 * share)), terms=shape((2, share), F32))
+        )
+        | far(out_grad=out_grad)
+        | near(**orders),
+        near(
+            qkv_low=shape((length, 3 * share)),
+            terms=shape((2, share), F32),
+            out_share=shape(out_block),
+        )
         | far(whole=shape(whole)),
         dict(
+            grads=pltpu.VMEM((length, share), BF16),
+            placed_low=pltpu.VMEM((length, 3 * share), BF16),
             query_turn=pltpu.VMEM((length, share), F32),
             key_turn=pltpu.VMEM((length, share), F32),
             value_sum=pltpu.VMEM((length, share), F32),
             sums=pltpu.VMEM((8, length), F32),
             sums_landed=pltpu.VMEM((ranks - 1, 8, length), F32),
             landed=pltpu.VMEM(whole, BF16),
+            out_sum=sum_scratch(*out_block, owners),
         ),
-        15 + ranks - 1,
-        8,
-    )
-
-
-def input_back(qkv_low, qkv, hidden_grad, qkv_grad, strip_grad, number):
+        15 + 17 + ranks - 1,
+        16,
+    )
+
+
+def input_back(qkv_low, qkv, hidden_grad, out_share, qkv_grad, strip_grad, number):
     ranks, owners = lax.axis_size("ctx"), lax.axis_size("fsdp")
     size, width = hidden_grad.shape
     length = qkv_low.shape[0]
+    height = out_share.shape[0]
     qkv_block = (qkv_grad.shape[0] // owners, qkv_grad.shape[1])
     strip_block = (strip_grad.shape[0], width // owners)
 
     def body(r, copies, stores):
         group, owner = Group("ctx"), Group("fsdp")
-        fetches = [stores.start(r.qkv_low, r.act), stores.start(r.qkv, r.qkv_near)]
+        fetches = [
+            stores.start(r.qkv_low, r.act),
+            stores.start(r.qkv, r.qkv_near),
+            stores.start(r.out_share, r.out_part),
+        ]
         meet(group.peers() + owner.peers())
         item = Sum(Rows(r.part, ranks), *r.landings)
+        out_item = Sum(Strips(r.out_part, ranks), *r.out_landings)
         sums = [
-            Sum(Rows(scratch[0], owners), *scratch[2:], out)
-            for scratch, out in ((r.qkv_sum, r.qkv_share), (r.strip_sum, r.strip_share))
+            Sum(Chips(scratch[0], owners), *scratch[2:], out)
+            for scratch, out in ((r.strip_sum, r.strip_share), (r.qkv_sum, r.qkv_share))
         ]
         owned = owner_sum(
             owner,
             copies,
             stores,
-            [Rows(r.qkv_grad, owners), Strips(r.strip_grad, owners)],
+            [Strips(r.strip_grad, owners), Rows(r.qkv_grad, owners)],
             sums,
-            [r.qkv_sum[1], r.strip_sum[1]],
+            [r.strip_sum[1], r.qkv_sum[1]],
         )
-        next(owned)
         for fetch in fetches:
             fetch.wait()
-        weave(ctx_sum(group, copies, r.act, r.qkv_near, item, 512, True), owned)
+        next(owned)
+        weave(ctx_sum(group, copies, r.act, r.qkv_near, [item, out_item], 512, True), owned)
         r.input_grad[...] = r.hidden_grad[...] + item.total(group)
+        r.out_mine[...] = low(out_item.total(group))
         finish(owned)
         copies.drain()
 
     return launch(
         number,
         body,
-        far(qkv_low=qkv_low, qkv=qkv, qkv_grad=qkv_grad, strip_grad=strip_grad)
+        far(
+            qkv_low=qkv_low, qkv=qkv, out_share=out_share, qkv_grad=qkv_grad, strip_grad=strip_grad
+        )
         | near(hidden_grad=hidden_grad),
         near(
             input_grad=shape((size, width), F32),
+            out_mine=shape((height, width // ranks)),
             qkv_share=shape(qkv_block),
             strip_share=shape(strip_block),
         ),
@@ -1084,11 +1144,13 @@
             qkv_near=pltpu.VMEM(qkv.shape, BF16),
             part=pltpu.VMEM((length, width), BF16),
             landings=landing(size, width, True),
+            out_part=pltpu.VMEM(out_share.shape, BF16),
+            out_landings=landing(height, width // ranks, True),
             qkv_sum=sum_scratch(*qkv_block, owners),
             strip_sum=sum_scratch(*strip_block, owners),
         ),
-        17 + 34,
-        2 + 16,
+        34 + 34,
+        3 + 16,
     )
 
 
@@ -1122,6 +1184,57 @@
         8 * count,
     )
     return [getattr(outs, "whole_" + name) for name in names]
+
+
+def unfold_kernel(units, shares, gate, up):
+    size, room = gate.shape[0], shares.shape[1] // 2
+    tail = units // 128 * 128
+    for i, out in enumerate((gate, up)):
+        span = pl.ds(i * room, room)
+        left = shares[pl.ds(0, size), span].astype(F32)
+        right = pltpu.roll(shares[pl.ds(size, size), span].astype(F32), units - tail, 1)
+        inside = lax.broadcasted_iota(jnp.int32, (size, 128), 1) < units - tail
+        out[:, pl.ds(0, tail)] = left[:, :tail]
+        out[:, pl.ds(tail, 128)] = jnp.where(inside, left[:, tail : tail + 128], right[:, :128])
+        out[:, pl.ds(tail + 128, tail)] = right[:, 128 : tail + 128]
+
+
+def unfold(shares, units):
+    ranks = lax.axis_size("ctx")
+    size = shares.shape[0] // ranks
+    return pl.pallas_call(
+        functools.partial(unfold_kernel, units),
+        grid=(ranks // 2,),
+        in_specs=[pl.BlockSpec((2 * size, shares.shape[1]), lambda i: (i, 0))],
+        out_specs=[pl.BlockSpec((size, 2 * units), lambda i: (0, i))] * 2,
+        out_shape=[shape((size, ranks * units), F32)] * 2,
+        compiler_params=pltpu.CompilerParams(vmem_limit_bytes=ROOM),
+    )(shares)
+
+
+def widen_kernel(qkv, out, down, query_out, key_out, value_out, out_out, down_out):
+    share = out.shape[1]
+    for i, ref in enumerate((query_out, key_out, value_out)):
+        ref[...] = qkv[:, pl.ds(i * share, share)].astype(F32)
+    out_out[...] = out[...].astype(F32)
+    down_out[...] = down[...].astype(F32)
+
+
+def widen(qkv, out, down):
+    ranks = lax.axis_size("ctx")
+    share = out.shape[1]
+    heights = [part.shape[0] // ranks for part in (qkv, qkv, qkv, out, down)]
+    return pl.pallas_call(
+        widen_kernel,
+        grid=(ranks,),
+        in_specs=[
+            pl.BlockSpec((part.shape[0] // ranks, part.shape[1]), lambda i: (i, 0))
+            for part in (qkv, out, down)
+        ],
+        out_specs=[pl.BlockSpec((height, share), lambda i: (0, i)) for height in heights],
+        out_shape=[shape((height, ranks * share), F32) for height in heights],
+        compiler_params=pltpu.CompilerParams(vmem_limit_bytes=ROOM),
+    )(qkv, out, down)
 
 
 def body(
@@ -1155,7 +1268,8 @@
     positions = (
         blocks[:, None] * block_len + jnp.arange(block_len, dtype=jnp.int32)[None, :]
     ).reshape(-1)
-    cosine, sine = angles(positions)
+    orders = dict(key_pos=positions[:, None], query_pos=positions[None, :])
+    cosine, sine = angles(2 * ranks * block_len)
 
     def cut(weight, size):
         return lax.dynamic_slice_in_dim(weight, rank * size, size, axis=1)
@@ -1182,63 +1296,50 @@
         for k in range(2)
     ]
     axes = ("ctx", "fsdp")
-    tall = jnp.concatenate([out_weight, down_weight], axis=0)
     pieces = []
     for k, route in enumerate(routes):
         target = 2 * rank + (odd ^ k)
-        strips = lax.dynamic_slice_in_dim(tall, target * strip, strip, axis=1)
+        strips = lax.dynamic_slice_in_dim(down_weight, target * strip, strip, axis=1)
         pieces.append(lax.ppermute(strips, axes, route))
 
     def in_order(pair):
         return jnp.where(odd == 0, pair[0], pair[1]), jnp.where(odd == 0, pair[1], pair[0])
 
     low_piece, high_piece = in_order(pieces)
-    out_size = out_weight.shape[0]
     strips = jnp.concatenate(
-        [
-            low_piece[:out_size],
-            high_piece[:out_size],
-            low_piece[out_size:],
-            high_piece[out_size:],
-            jnp.zeros((room - units, strip), BF16),
-        ],
-        axis=0,
+        [low_piece, high_piece, jnp.zeros((room - units, strip), BF16)], axis=0
     )
 
     front = attend(
-        inputs,
-        qkv_mine,
-        gains_mine,
-        strips[:share],
-        jnp.concatenate([wide(gate_weight), wide(up_weight)], axis=1),
-        cosine,
-        sine,
-        positions,
-        1,
-    )
-    fed = feed_in(
-        front.mixed, front.out_rows, inputs, front.scales, front.gate_up, strips[share:], 2
-    )
-    back = feed_out(
-        fed.product, fed.down_rows, fed.pre, fed.hidden, cotangent[0], front.scales, 3
-    )
-    gate_up_grad = low(outer_sum(fed.whole, back.both_low))
-    down_grad = low(outer_sum(fed.product, back.whole))
+        inputs, qkv_mine, gains_mine, out_weight, wide(gate_weight), cosine, sine, orders, 1
+    )
+    fed = feed(
+        front.hidden,
+        front.hidden_low,
+        front.gate,
+        wide(up_weight),
+        strips,
+        cotangent[0],
+        front.scales,
+        2,
+    )
+    gate_up_grad = low(outer_sum(fed.whole_hidden, fed.both_low))
     inner = hidden_back(
-        back.both_low,
-        front.gate_up,
+        fed.both_low,
+        front.gate,
+        fed.up,
         cotangent[0],
-        fed.attn_raw,
+        front.attn_raw,
         front.scales,
-        front.out_rows,
+        front.out_whole,
         gate_up_grad,
-        down_grad,
-        4,
-    )
-    out_rows_grad = low(outer_sum(front.mixed, inner.whole))
+        3,
+    )
+    out_grad = low(outer_sum(front.mixed_rows, inner.attn_low))
     outer = attend_back(
-        front, inner.mixed_grad, cosine, sine, positions, inner.gate_up_share, 5
-    )
+        front, inner.mixed_grad, cosine, sine, orders, inner.gate_up_share, out_grad, 4
+    )
+    down_grad = low(outer_sum(fed.product, fed.whole_down))
     qkv_grad = low(outer_sum(front.whole, outer.qkv_low))
 
     def placed(term):
@@ -1246,47 +1347,30 @@
             jnp.zeros((width,), F32), term, rank * share, axis=0
         )
 
-    gain_terms = low(jnp.stack([placed(outer.terms[0]), placed(outer.terms[1]), inner.attn_term[0], back.feed_term[0]]))
-    strip_grads = jnp.concatenate([out_rows_grad, jnp.pad(gain_terms, ((0, 28), (0, 0)))], axis=0)
+    gain_terms = low(jnp.stack([placed(outer.terms[0]), placed(outer.terms[1]), inner.attn_term[0], fed.feed_term[0]]))
+    strip_grads = jnp.concatenate([down_grad, jnp.pad(gain_terms, ((0, 28), (0, 0)))], axis=0)
     last = input_back(
-        outer.qkv_low, front.qkv, inner.hidden_grad, qkv_grad, strip_grads, 6
-    )
-    out_share, gains_share = last.strip_share[:share], last.strip_share[share:]
-    down_share = inner.down_share
+        outer.qkv_low, front.qkv, inner.hidden_grad, outer.out_share, qkv_grad, strip_grads, 5
+    )
     down_size = down_weight.shape[0]
-    by_owner = [
-        jnp.concatenate(
-            [
-                out_share[j * out_size : (j + 1) * out_size],
-                down_share[j * down_size : (j + 1) * down_size],
-            ],
-            axis=0,
-        )
-        for j in range(2)
-    ]
+    by_owner = [last.strip_share[j * down_size : (j + 1) * down_size] for j in range(2)]
+    gains_share = last.strip_share[room:]
     by_route = in_order(by_owner)
     returned = [
         lax.ppermute(piece, axes, [(b, a) for a, b in route])
         for piece, route in zip(by_route, routes)
     ]
-    tall_share = jnp.concatenate(in_order(returned), axis=1)
-
-    qkv_all, tall_all, gains_all = spread([last.qkv_share, tall_share, gains_share], 7)
-
-    def side_by_side(parts, size, at):
-        columns = parts.reshape(ranks, -1, parts.shape[-1])[:, :, at : at + size]
-        return columns.transpose(1, 0, 2).reshape(columns.shape[1], -1).astype(F32)
-
-    gate_share, up_share = (side_by_side(outer.whole, units, at) for at in (0, room))
-    query_share, key_share, value_share = (
-        side_by_side(qkv_all, share, i * share) for i in range(3)
-    )
-    tall_whole = side_by_side(tall_all, share, 0)
-    out_share, down_share = tall_whole[:out_size], tall_whole[out_size:]
-
+    down_share = jnp.concatenate(in_order(returned), axis=1)
+
+    qkv_all, out_all, down_all, gains_all = spread(
+        [last.qkv_share, last.out_mine, down_share, gains_share], 6
+    )
+
+    gate_share, up_share = unfold(outer.whole, units)
+    query_share, key_share, value_share, out_share, down_share = widen(qkv_all, out_all, down_all)
     mine = jnp.sum(gains_all.reshape(ranks, -1, strip)[:, :4].astype(F32), axis=0)
     return (
-        back.result[None],
+        fed.result[None],
         last.input_grad[None],
         query_share,
         key_share,

time: 541 us -> 480 us (0.89)
  Pallas kernels: 452 us -> 414 us
  local copies, waits for them, and re-layouts: 29.5 us -> 14.4 us
  other arithmetic: 15.7 us -> 7.45 us
    pallas_call x7 -> x6, Pallas kernels: 452 us -> 401 us  [launch(): pl.pallas_call(kernel, out_shape=[out for out, _ in outs.values()], in_sp...]
    pallas_call x0 -> x2, Pallas kernels: none -> 12.3 us  [the longest x1 7.34 us: widen(): pl.pallas_call(widen_kernel, grid=(ranks,), in_specs=[pl.BlockSpec((part....]
    unnamed x47 -> x32, local copies, waits for them, and re-layouts: 11.8 us -> 3.6 us
  transfers between devices with their start and end apart: 4 -> 4, of which waited for: 0 -> 0; matrix products, arithmetic and copies ran while one was open for 5% -> 2% of each run, Pallas kernels for 0% -> 21%
where the time goes in v1:
time: 480 us; the launch traced here: 474 us
  Pallas kernels  414 us (86%)
  matrix products  26.9 us (6%)
  local copies, waits for them, and re-layouts  14.4 us (3%)
  starting transfers between devices  10.1 us (2%)
  other arithmetic  7.45 us (2%)
    pallas_call x6, Pallas kernels, launch(): pl.pallas_call(kernel, out_shape=[out for out, _ in outs.values()], in_sp...  401 us
    dot_general x4, matrix products, outer_sum(): lax.dot_general(left, right, (((0,), (0,)), ((), ())), preferred_element_...  26.9 us
  transfers between devices with their start and end apart: 4, of which 0 were waited for; matrix products, arithmetic and copies ran while one was open for 2% of the time, Pallas kernels for 21%

profile of v1, /device:TPU:2, one launch (start us, length us, event | category | flops | bytes accessed | tf_op | source)
XLA Modules:
  0.0 473.8 jit_solution(7157967614683991144)
XLA Ops:
  0.7 1.1 constant_dynamic-slice_fusion.1
  1.8 3.8 collective-permute-start
  6.8 1.3 add.75.refs_7_.refs_12_
  8.9 1.1 constant_dynamic-slice_fusion.2
  10.9 0.9 constant_dynamic-slice_fusion.4
  14.5 92.8 %shard_map.255 = (bf16[1024,2048]{1,0:T(8,128)(2,1)}, bf16[2048,768]{1,0:T(8,128)(2,1)}, bf16[2048,2048]{1,0:T(8,128)(2,1)}, bf16[2048,768]{1,0:T(8,128)(2,1)}, ...) custom-call(bf16[128,2048]{1,0:T(8,128)(2,1)} %bitcast.29, ...), custom_call_target="tpu_custom_call" | custom-call | tf_op jit(solution)/shard_map/pallas_call | solution.py:418
  107.3 0.8 maximum_maximum_fusion.refs_4_
  108.2 121.5 %shard_map.256 = (bf16[1024,2048]{1,0:T(8,128)(2,1)}, bf16[1024,2048]{1,0:T(8,128)(2,1)}, bf16[2048,768]{1,0:T(8,128)(2,1)}, bf16[768,2048]{1,0:T(8,128)(2,1)}, ...) custom-call(bf16[2048,768]{1,0:T(8,128)(2,1)} %get-tuple-element.59.refs_, ...), custom_call_target="tpu_custom_call" | custom-call | tf_op jit(solution)/shard_map/pallas_call | solution.py:418
  229.7 11.6 %convolution_convert_fusion.refs_4_ = bf16[2048,1536]{1,0:T(8,128)(2,1)} fusion(bf16[1024,2048]{1,0:T(8,128)(2,1)} %get-tuple-element.73, bf16[1024,1536]{1,0:T(8,128)(2,1)} %get-tuple-element.70.refs_0_), kind=kOutput, calls=%fused_computation | convolution fusion | flops 6445596672 | bytes 13631488 | tf_op jit(solution)/shard_map/dot_general | solution.py:33
  241.3 52.4 %shard_map.257 = (f32[128,2048]{1,0:T(8,128)}, f32[1,2048]{1,0:T(1,128)}, bf16[128,2048]{1,0:T(8,128)(2,1)}, bf16[1024,256]{1,0:T(8,128)(2,1)}, bf16[128,1536]{1,0:T(8,128)(2,1)}) custom-call(bf16[1024,1536]{1,0:T(8,128)(2,1)} %get-tuple-element.70.refs_0_, bf16[2048,768]{1,0:T(8,128)(2,1)} %get-tuple-element.59.refs_0_.refs_1_, ...), custom_call_target="tpu_custom_call" | custom-call | tf_op jit(solution)/shard_map/pallas_call | solution.py:418
  293.7 6.7 %convolution_convert_fusion.1.refs_11_ = bf16[2048,2048]{1,0:T(8,128)(2,1)} fusion(bf16[128,2048]{1,0:T(8,128)(2,1)S(1)} %copy-done.4, bf16[128,2048]{1,0:T(8,128)(2,1)} %get-tuple-element.78), kind=kOutput, calls=%fused_computation.1 | convolution fusion | flops 1077936128 | bytes 9437184 | tf_op jit(solution)/shard_map/dot_general | solution.py:33
  300.4 49.4 %shard_map.258 = (bf16[1024,768]{1,0:T(8,128)(2,1)}, f32[2,256]{1,0:T(2,128)}, bf16[128,2048]{1,0:T(8,128)(2,1)}, bf16[1024,1536]{1,0:T(8,128)(2,1)}) custom-call(bf16[1024,256]{1,0:T(8,128)(2,1)} %get-tuple-element.64.refs_0_, bf16[1024,256]{1,0:T(8,128)(2,1)} %get-tuple-element.65.refs_1_, bf16[1024,256]{1,0:T(8,128)(2,1)} %get-tuple-element.66.refs_2_, ...), custom_call_target="tpu_custom_call" | custom-call | tf_op jit(solution)/shard_map/pallas_call | solution.py:418
  351.3 3.7 convolution_convert_fusion.2
  355.1 2.1 pad_maximum_fusion.refs_4_
  357.2 1.8 copy-done.12
  358.9 5.0 %convolution_convert_fusion.3.refs_3_ = bf16[2048,768]{1,0:T(8,128)(2,1)} fusion(bf16[1024,2048]{1,0:T(8,128)(2,1)S(1)} %copy-done.12, bf16[1024,768]{1,0:T(8,128)(2,1)S(1)} %copy-done.2), kind=kOutput, calls=%fused_computation.3 | convolution fusion | flops 3222798336 | bytes 8912896 | tf_op jit(solution)/shard_map/dot_general | solution.py:33
  363.9 45.7 %shard_map.259 = (f32[128,2048]{1,0:T(8,128)}, bf16[128,256]{1,0:T(8,128)(2,1)}, bf16[128,768]{1,0:T(8,128)(2,1)}, bf16[800,128]{1,0:T(8,128)(2,1)}) custom-call(bf16[1024,768]{1,0:T(8,128)(2,1)} %get-tuple-element.79.refs_0_, bf16[2048,768]{1,0:T(8,128)(2,1)} %get-tuple-element.80.refs_1_, bf16[128,2048]{1,0:T(8,128)(2,1)} %get-tuple-element.81.refs_2_, ...), custom_call_target="tpu_custom_call" | custom-call | tf_op jit(solution)/shard_map/pallas_call | solution.py:418
  409.7 1.0 broadcast_select_fusion.3
  410.6 6.0 %collective-permute-start.2 = (bf16[352,128]{1,0:T(8,128)(2,1)S(1)}, bf16[352,128]{1,0:T(8,128)(2,1)S(1)}, u32[]{:S(2)}, u32[]{:S(2)}) collective-permute-start(bf16[352,128]{1,0:T(8,128)(2,1)S(1)} %get-tuple-element.107), channel_id=1, source_target_pairs={{0,0},{1,1},{16,2},{17,3},{32,4},{33,5},{48,6},{49,7},{64,8},{65,9... | collective-permute-start | bytes 270344 | tf_op jit(solution)/shard_map/ppermute | solution.py:1360
  416.7 1.3 slice.34.refs_3_
  418.0 5.0 %shard_map.262 = (f32[128,5632]{1,0:T(8,128)}, f32[128,5632]{1,0:T(8,128)}) custom-call(bf16[1024,1536]{1,0:T(8,128)(2,1)} %get-tuple-element.100.shares), custom_call_target="tpu_custom_call" | custom-call | tf_op jit(solution)/shard_map/pallas_call | solution.py:1205
  423.7 39.5 %shard_map.260 = (bf16[1024,768]{1,0:T(8,128)(2,1)}, bf16[1024,256]{1,0:T(8,128)(2,1)}, bf16[2816,256]{1,0:T(8,128)(2,1)}, bf16[256,128]{1,0:T(8,128)(2,1)}) custom-call(bf16[128,768]{1,0:T(8,128)(2,1)} %get-tuple-element.90.refs_0_, bf16[128,256]{1,0:T(8,128)(2,1)} %get-tuple-element.91.refs_1_, bf16[352,256]{1,0:T(8,128)(2,1)} %pad_maximum_fusion.2.refs_2_, ...), custom_call_target="tpu_custom_call" | custom-call | tf_op jit(solution)/shard_map/pallas_call | solution.py:418
  464.4 7.3 %shard_map.261 = (f32[128,2048]{1,0:T(8,128)}, f32[128,2048]{1,0:T(8,128)}, f32[128,2048]{1,0:T(8,128)}, f32[128,2048]{1,0:T(8,128)}, f32[352,2048]{1,0:T(8,128)}) custom-call(bf16[1024,768]{1,0:T(8,128)(2,1)} %get-tuple-element.93.qkv, bf16[1024,256]{1,0:T(8,128)(2,1)} %get-tuple-element.94.out, bf16[2816,256]{1,0:T(8,128)(2,1)} %get-tuple-element.95.down), custom_call_target="tpu_custom_call" | custom-call | tf_op jit(solution)/shard_map/pallas_call | solution.py:1227
  472.6 1.0 copy.40
  (61 shorter events, 10.0 us)
Async XLA Ops:
  0.6 8.1 %copy-start = (bf16[128,5632]{1,0:T(8,128)(2,1)S(1)}, bf16[128,5632]{1,0:T(8,128)(2,1)}, u32[]{:S(2)}) copy-start(bf16[128,5632]{1,0:T(8,128)(2,1)} %param.22) | copy-start | bytes 4325380
  0.7 13.2 %copy-start.11 = (bf16[128]{0:T(256)(128)(2,1)S(1)}, bf16[128]{0:T(256)(128)(2,1)}, u32[]{:S(2)}) copy-start(bf16[128]{0:T(256)(128)(2,1)} %param.25) | copy-start | bytes 772
  0.7 13.2 %copy-start.10 = (bf16[128]{0:T(256)(128)(2,1)S(1)}, bf16[128]{0:T(256)(128)(2,1)}, u32[]{:S(2)}) copy-start(bf16[128]{0:T(256)(128)(2,1)} %param.26) | copy-start | bytes 772
  0.7 13.2 %copy-start.9 = (bf16[128]{0:T(256)(128)(2,1)S(1)}, bf16[128]{0:T(256)(128)(2,1)}, u32[]{:S(2)}) copy-start(bf16[128]{0:T(256)(128)(2,1)} %param.27) | copy-start | bytes 772
  0.7 13.1 %copy-start.8 = (bf16[128]{0:T(256)(128)(2,1)S(1)}, bf16[128]{0:T(256)(128)(2,1)}, u32[]{:S(2)}) copy-start(bf16[128]{0:T(256)(128)(2,1)} %param.28) | copy-start | bytes 772
  1.8 105.5 %collective-permute-start = (bf16[352,128]{1,0:T(8,128)(2,1)S(1)}, bf16[352,128]{1,0:T(8,128)(2,1)S(1)}, u32[]{:S(2)}, u32[]{:S(2)}) collective-permute-start(bf16[352,128]{1,0:T(8,128)(2,1)S(1)} %get-tuple-element.105), channel_id=1, source_target_pairs={{0,0},{1,1},{2,16},{3,17},{4,32},{5,33},{6,48},{7,49},{8,64},{9,65... | collective-permute-start | bytes 270344 | tf_op jit(solution)/shard_map/ppermute | solution.py:1303
  5.6 101.7 %collective-permute-start.1 = (bf16[352,128]{1,0:T(8,128)(2,1)S(1)}, bf16[352,128]{1,0:T(8,128)(2,1)S(1)}, u32[]{:S(2)}, u32[]{:S(2)}) collective-permute-start(bf16[352,128]{1,0:T(8,128)(2,1)S(1)} %get-tuple-element.106), channel_id=1, source_target_pairs={{0,1},{1,0},{2,17},{3,16},{4,33},{5,32},{6,49},{7,48},{8,65},{9,64... | collective-permute-start | bytes 270344 | tf_op jit(solution)/shard_map/ppermute | solution.py:1303
  241.3 52.4 %copy-start.4 = (bf16[128,2048]{1,0:T(8,128)(2,1)S(1)}, bf16[128,2048]{1,0:T(8,128)(2,1)}, u32[]{:S(2)}) copy-start(bf16[128,2048]{1,0:T(8,128)(2,1)} %get-tuple-element.77) | copy-start | bytes 1572868
  300.4 50.9 %copy-start.7 = (f32[1,2048]{1,0:T(1,128)S(1)}, f32[1,2048]{1,0:T(1,128)}, u32[]{:S(2)}) copy-start(f32[1,2048]{1,0:T(1,128)} %get-tuple-element.86) | copy-start | bytes 24580
  300.4 50.9 %copy-start.6 = (f32[1,2048]{1,0:T(1,128)S(1)}, f32[1,2048]{1,0:T(1,128)}, u32[]{:S(2)}) copy-start(f32[1,2048]{1,0:T(1,128)} %get-tuple-element.87) | copy-start | bytes 24580
  300.4 50.9 %copy-start.13 = (bf16[1024,2048]{1,0:T(8,128)(2,1)S(1)}, bf16[1024,2048]{1,0:T(8,128)(2,1)}, u32[]{:S(2)}) copy-start(bf16[1024,2048]{1,0:T(8,128)(2,1)} %get-tuple-element.84) | copy-start | bytes 12582916
  300.4 50.9 %copy-start.14 = (bf16[1024,768]{1,0:T(8,128)(2,1)S(1)}, bf16[1024,768]{1,0:T(8,128)(2,1)}, u32[]{:S(2)}) copy-start(bf16[1024,768]{1,0:T(8,128)(2,1)} %get-tuple-element.83) | copy-start | bytes 4718596
  355.1 2.1 copy-start.2
  355.1 3.8 copy-start.12
  410.6 12.4 %collective-permute-start.2 = (bf16[352,128]{1,0:T(8,128)(2,1)S(1)}, bf16[352,128]{1,0:T(8,128)(2,1)S(1)}, u32[]{:S(2)}, u32[]{:S(2)}) collective-permute-start(bf16[352,128]{1,0:T(8,128)(2,1)S(1)} %get-tuple-element.107), channel_id=1, source_target_pairs={{0,0},{1,1},{16,2},{17,3},{32,4},{33,5},{48,6},{49,7},{64,8},{65,9... | collective-permute-start | bytes 270344 | tf_op jit(solution)/shard_map/ppermute | solution.py:1360
  416.6 6.4 %collective-permute-start.3 = (bf16[352,128]{1,0:T(8,128)(2,1)S(1)}, bf16[352,128]{1,0:T(8,128)(2,1)S(1)}, u32[]{:S(2)}, u32[]{:S(2)}) collective-permute-start(bf16[352,128]{1,0:T(8,128)(2,1)S(1)} %get-tuple-element.108), channel_id=1, source_target_pairs={{1,0},{0,1},{17,2},{16,3},{33,4},{32,5},{49,6},{48,7},{65,8},{64,9... | collective-permute-start | bytes 270344 | tf_op jit(solution)/shard_map/ppermute | solution.py:1360
  423.0 48.8 %copy-start.5 = (bf16[128,2048]{1,0:T(8,128)(2,1)S(1)}, bf16[128,2048]{1,0:T(8,128)(2,1)}, u32[]{:S(2)}) copy-start(bf16[128,2048]{1,0:T(8,128)(2,1)} %get-tuple-element.63) | copy-start | bytes 1572868
  423.0 49.6 %copy-start.3 = (f32[128,2048]{1,0:T(8,128)S(1)}, f32[128,2048]{1,0:T(8,128)}, u32[]{:S(2)}) copy-start(f32[128,2048]{1,0:T(8,128)} %get-tuple-element.89) | copy-start | bytes 3145732
  464.4 9.1 %copy-start.1 = (bf16[128,5632]{1,0:T(8,128)(2,1)S(1)}, bf16[128,5632]{1,0:T(8,128)(2,1)}, u32[]{:S(2)}) copy-start(bf16[128,5632]{1,0:T(8,128)(2,1)} %param.22) | copy-start | bytes 4325380

commit v2 on v1

--- a/solution.py
+++ b/solution.py
@@ -296,25 +296,25 @@
                 started.append(copies.start(view, window(item.side, (side, i), lo, hi), peer))
         return started
 
-    prepare(True, 2)
+    prepare((True, 2))
     far_other = send_far(0)
     edges = {2: send_edges(2)}
     yield
-    prepare(False, 2)
+    prepare((False, 2))
     arrived(edges[2])
     add_edges(2)
     far_same = send_far(1)
     yield
+    prepare((True, 1), (True, 3))
     for step in (1, 3):
-        prepare(True, step)
         edges[step] = send_edges(step)
     yield
     near_other = send_near(0, far_other)
     yield
-    prepare(True, 0)
+    prepare((True, 0))
     edges[0] = send_edges(0)
+    prepare((False, 1), (False, 3))
     for step in (1, 3):
-        prepare(False, step)
         arrived(edges[step])
         add_edges(step)
     near_same = send_near(1, far_same)
@@ -327,7 +327,7 @@
         add(view, [window(item.side, (0, 0), lo, hi), window(item.side, (1, 0), lo, hi)])
         across.append(copies.start(view, window(item.cross, (0,), lo, hi), partner))
     yield
-    prepare(False, 0)
+    prepare((False, 0))
     yield
     arrived(near_same)
     arrived(across)
@@ -352,6 +352,15 @@
     yield
 
 
+class Made:
+    def __init__(self, left, right, given, owners):
+        self.left, self.right, self.given = left, right, given
+        self.width = left.shape[1] // owners
+
+    def block(self, index):
+        return low(outer_sum(self.left[:, rows_at(index, self.width)], self.right[...]))
+
+
 def owner_sum(owner, copies, stores, sources, sums, from_sibling):
     sibling = {owner.axis: owner.sibling}
     turn = 1 - 2 * owner.core
@@ -359,20 +368,26 @@
     for step in (2, 1, 3, 0):
         for other in (True, False):
             index, number = owner.at(other, step), len(waits)
-            waits[other, step] = [
-                (
-                    stores.start(source.block(index), item.parts.block(index)),
-                    copies.start(source.block(index + turn), landed.at[number], sibling),
-                    landed.at[number],
-                )
-                for source, item, landed in zip(sources, sums, from_sibling)
-            ]
-
-    def prepare(other, step):
-        for (fetch, give, landed), item in zip(waits[other, step], sums):
-            fetch.wait()
-            give.wait_recv()
-            add(item.parts.block(owner.at(other, step)), [landed])
+            waits[other, step] = []
+            for source, item, landed in zip(sources, sums, from_sibling):
+                fetch, place = None, landed.at[number]
+                if isinstance(source, Made):
+                    given = source.given.at[number]
+                    given[...] = source.block(index + turn)
+                    give = copies.start(given, place, sibling)
+                    item.parts.block(index)[...] = source.block(index)
+                else:
+                    fetch = stores.start(source.block(index), item.parts.block(index))
+                    give = copies.start(source.block(index + turn), place, sibling)
+                waits[other, step].append((fetch, give, place))
+
+    def prepare(*places):
+        for place in places:
+            for (fetch, give, landed), item in zip(waits[place], sums):
+                if fetch is not None:
+                    fetch.wait()
+                give.wait_recv()
+                add(item.parts.block(owner.at(*place)), [landed])
 
     yield
     yield from ring_scatter(owner, copies, sums, prepare)
@@ -495,15 +510,15 @@
 def ctx_sum(group, copies, act, weight, items, tile, transposed):
     parts = items[0].parts
 
-    def prepare(other, step):
-        rows = rows_at(group.at(other, step), parts.rows)
-        tiles(parts.ref, [rows], [act[rows, :]], weight, tile, transposed)
+    def prepare(*places):
+        rows = [rows_at(group.at(other, step), parts.rows) for other, step in places]
+        tiles(parts.ref, rows, [act[at, :] for at in rows], weight, tile, transposed)
 
     return ring_scatter(group, copies, items, prepare, True)
 
 
 def weave(main, stream):
-    for step in "000110101010101":
+    for step in "0001110101010101":
         next(stream if step == "1" else main)
 
 
@@ -877,12 +892,12 @@
     )
 
 
-def hidden_back(both_low, gate, up, cotangent, attn_raw, scales, out_whole, gate_up_grad, number):
+def hidden_back(both_low, gate, up, cotangent, attn_raw, scales, out_whole, whole_hidden, number):
     ranks, owners = lax.axis_size("ctx"), lax.axis_size("fsdp")
     size, width = attn_raw.shape
     length, both = both_low.shape
     room, share = both // 2, width // ranks
-    gate_up_block = (gate_up_grad.shape[0] // owners, both)
+    gate_up_block = (width // owners, both)
 
     def body(r, copies, stores):
         group, owner = Group("ctx"), Group("fsdp")
@@ -892,18 +907,25 @@
             stores.start(r.gate, r.gate_up_near.at[:, pl.ds(0, room)]),
             stores.start(r.up, r.gate_up_near.at[:, pl.ds(room, room)]),
         ]
+        rows_fetch = stores.start(r.whole_hidden, r.rows_near)
         out_fetch = stores.start(r.out_whole, r.out_near)
         meet([{"ctx": other} for other in others] + owner.peers())
         item = Sum(Rows(r.part, ranks), *r.landings)
         part, from_sibling, *places = r.gate_up_sum
         own = Sum(Chips(part, owners), *places, r.gate_up_share)
         owned = owner_sum(
-            owner, copies, stores, [Rows(r.gate_up_grad, owners)], [own], [from_sibling]
+            owner,
+            copies,
+            stores,
+            [Made(r.rows_near, r.act, r.given, owners)],
+            [own],
+            [from_sibling],
         )
         for fetch in fetches:
             fetch.wait()
-        next(owned)
-        weave(ctx_sum(group, copies, r.act, r.gate_up_near, [item], 512, True), owned)
+        rows_fetch.wait()
+        main = ctx_sum(group, copies, r.act, r.gate_up_near, [item], 512, True)
+        weave(main, owned)
         hidden_grad = r.cotangent[...].astype(F32) + item.total(group)
         r.hidden_grad[...] = hidden_grad
         unit, inverse = norm(r.attn_raw[...])
@@ -928,7 +950,7 @@
     return launch(
         number,
         body,
-        far(both_low=both_low, gate=gate, up=up, out_whole=out_whole, gate_up_grad=gate_up_grad)
+        far(both_low=both_low, gate=gate, up=up, out_whole=out_whole, whole_hidden=whole_hidden)
         | near(cotangent=cotangent, attn_raw=attn_raw, scales=scales),
         near(
             hidden_grad=shape((size, width), F32),
@@ -943,6 +965,8 @@
             out_near=pltpu.VMEM(out_whole.shape, BF16),
             part=pltpu.VMEM((length, width), BF16),
             landings=landing(size, width, True),
+            rows_near=pltpu.VMEM((length, width), BF16),
+            given=pltpu.VMEM((owners // 2, *gate_up_block), BF16),
             mixed_out=pltpu.VMEM((ranks - 1, size, share), BF16),
             mixed_landed=pltpu.VMEM((length, share), BF16),
             gate_up_sum=sum_scratch(*gate_up_block, owners),
@@ -952,12 +976,13 @@
     )
 
 
-def attend_back(front, mixed_grad, cosine, sine, orders, gate_up_share, out_grad, number):
+def attend_back(front, mixed_grad, cosine, sine, orders, gate_up_share, attn_low, number):
     ranks, owners = lax.axis_size("ctx"), lax.axis_size("fsdp")
     length, share = mixed_grad.shape
     lanes, chunk = 2 * HD, 256
     whole = (ranks * gate_up_share.shape[0], gate_up_share.shape[1])
-    out_block = (out_grad.shape[0] // owners, out_grad.shape[1])
+    size, width = attn_low.shape
+    out_block = (width // owners, width)
 
     def body(r, copies, stores):
         group, owner = Group("ctx"), Group("fsdp")
@@ -969,7 +994,14 @@
         stores.start(r.block, stored.block(group.me))
         part, from_sibling, *places = r.out_sum
         own = Sum(Chips(part, owners), *places, r.out_share)
-        owned = owner_sum(owner, copies, stores, [Rows(r.out_grad, owners)], [own], [from_sibling])
+        owned = owner_sum(
+            owner,
+            copies,
+            stores,
+            [Made(r.mixed_rows, r.attn_low, r.given, owners)],
+            [own],
+            [from_sibling],
+        )
         next(owned)
         next(owned)
         r.key_turn[...] = jnp.zeros_like(r.key_turn)
@@ -1062,8 +1094,9 @@
             cosine=cosine,
             sine=sine,
             block=gate_up_share,
+            mixed_rows=front.mixed_rows,
+            attn_low=attn_low,
         )
-        | far(out_grad=out_grad)
         | near(**orders),
         near(
             qkv_low=shape((length, 3 * share)),
@@ -1072,6 +1105,7 @@
         )
         | far(whole=shape(whole)),
         dict(
+            given=pltpu.VMEM((owners // 2, *out_block), BF16),
             grads=pltpu.VMEM((length, share), BF16),
             placed_low=pltpu.VMEM((length, 3 * share), BF16),
             query_turn=pltpu.VMEM((length, share), F32),
@@ -1087,12 +1121,12 @@
     )
 
 
-def input_back(qkv_low, qkv, hidden_grad, out_share, qkv_grad, strip_grad, number):
+def input_back(qkv_low, qkv, hidden_grad, out_share, whole, strip_grad, number):
     ranks, owners = lax.axis_size("ctx"), lax.axis_size("fsdp")
     size, width = hidden_grad.shape
     length = qkv_low.shape[0]
     height = out_share.shape[0]
-    qkv_block = (qkv_grad.shape[0] // owners, qkv_grad.shape[1])
+    qkv_block = (width // owners, qkv_low.shape[1])
     strip_block = (strip_grad.shape[0], width // owners)
 
     def body(r, copies, stores):
@@ -1101,6 +1135,7 @@
             stores.start(r.qkv_low, r.act),
             stores.start(r.qkv, r.qkv_near),
             stores.start(r.out_share, r.out_part),
+            stores.start(r.whole, r.rows_near),
         ]
         meet(group.peers() + owner.peers())
         item = Sum(Rows(r.part, ranks), *r.landings)
@@ -1113,13 +1148,12 @@
             owner,
             copies,
             stores,
-            [Strips(r.strip_grad, owners), Rows(r.qkv_grad, owners)],
+            [Strips(r.strip_grad, owners), Made(r.rows_near, r.act, r.given, owners)],
             sums,
             [r.strip_sum[1], r.qkv_sum[1]],
         )
         for fetch in fetches:
             fetch.wait()
-        next(owned)
         weave(ctx_sum(group, copies, r.act, r.qkv_near, [item, out_item], 512, True), owned)
         r.input_grad[...] = r.hidden_grad[...] + item.total(group)
         r.out_mine[...] = low(out_item.total(group))
@@ -1130,7 +1164,7 @@
         number,
         body,
         far(
-            qkv_low=qkv_low, qkv=qkv, out_share=out_share, qkv_grad=qkv_grad, strip_grad=strip_grad
+            qkv_low=qkv_low, qkv=qkv, out_share=out_share, whole=whole, strip_grad=strip_grad
         )
         | near(hidden_grad=hidden_grad),
         near(
@@ -1144,13 +1178,15 @@
             qkv_near=pltpu.VMEM(qkv.shape, BF16),
             part=pltpu.VMEM((length, width), BF16),
             landings=landing(size, width, True),
+            rows_near=pltpu.VMEM((length, width), BF16),
+            given=pltpu.VMEM((owners // 2, *qkv_block), BF16),
             out_part=pltpu.VMEM(out_share.shape, BF16),
             out_landings=landing(height, width // ranks, True),
             qkv_sum=sum_scratch(*qkv_block, owners),
             strip_sum=sum_scratch(*strip_block, owners),
         ),
         34 + 34,
-        3 + 16,
+        4 + 16,
     )
 
 
@@ -1323,7 +1359,6 @@
         front.scales,
         2,
     )
-    gate_up_grad = low(outer_sum(fed.whole_hidden, fed.both_low))
     inner = hidden_back(
         fed.both_low,
         front.gate,
@@ -1332,15 +1367,13 @@
         front.attn_raw,
         front.scales,
         front.out_whole,
-        gate_up_grad,
+        fed.whole_hidden,
         3,
     )
-    out_grad = low(outer_sum(front.mixed_rows, inner.attn_low))
     outer = attend_back(
-        front, inner.mixed_grad, cosine, sine, orders, inner.gate_up_share, out_grad, 4
+        front, inner.mixed_grad, cosine, sine, orders, inner.gate_up_share, inner.attn_low, 4
     )
     down_grad = low(outer_sum(fed.product, fed.whole_down))
-    qkv_grad = low(outer_sum(front.whole, outer.qkv_low))
 
     def placed(term):
         return lax.dynamic_update_slice_in_dim(
@@ -1350,7 +1383,7 @@
     gain_terms = low(jnp.stack([placed(outer.terms[0]), placed(outer.terms[1]), inner.attn_term[0], fed.feed_term[0]]))
     strip_grads = jnp.concatenate([down_grad, jnp.pad(gain_terms, ((0, 28), (0, 0)))], axis=0)
     last = input_back(
-        outer.qkv_low, front.qkv, inner.hidden_grad, outer.out_share, qkv_grad, strip_grads, 5
+        outer.qkv_low, front.qkv, inner.hidden_grad, outer.out_share, front.whole, strip_grads, 5
     )
     down_size = down_weight.shape[0]
     by_owner = [last.strip_share[j * down_size : (j + 1) * down_size] for j in range(2)]

time: 480 us -> 471 us (0.981)
  matrix products: 26.9 us -> 3.69 us
  Pallas kernels: 414 us -> 426 us
    dot_general x4 -> x1, matrix products: 26.9 us -> 3.69 us  [outer_sum(): lax.dot_general(left, right, (((0,), (0,)), ((), ())), preferred_element_...]
    pallas_call x6, Pallas kernels: 401 us -> 414 us  [launch(): pl.pallas_call(kernel, out_shape=[out for out, _ in outs.values()], in_sp...]
where the time goes in v2:
time: 471 us; the launch traced here: 463 us
  Pallas kernels  426 us (90%)
  starting transfers between devices  12.6 us (3%)
  local copies, waits for them, and re-layouts  12.5 us (3%)
  other arithmetic  7.45 us (2%)
    pallas_call x6, Pallas kernels, launch(): pl.pallas_call(kernel, out_shape=[out for out, _ in outs.values()], in_sp...  414 us
  transfers between devices with their start and end apart: 4, of which 0 were waited for; matrix products, arithmetic and copies ran while one was open for 2% of the time, Pallas kernels for 21%

profile of v2, /device:TPU:2, one launch (start us, length us, event | category | flops | bytes accessed | tf_op | source)
XLA Modules:
  0.0 463.5 jit_solution(1915740515820599644)
XLA Ops:
  0.7 1.1 constant_dynamic-slice_fusion.1
  1.8 3.8 collective-permute-start
  6.8 1.3 add.75.refs_7_.refs_13_
  8.9 1.1 constant_dynamic-slice_fusion.2
  10.0 0.8 constant_dynamic-slice_fusion.6
  10.9 0.9 constant_dynamic-slice_fusion.4
  11.7 0.7 pad.16.refs_4_
  14.5 93.0 %shard_map.255 = (bf16[1024,2048]{1,0:T(8,128)(2,1)}, bf16[2048,768]{1,0:T(8,128)(2,1)}, bf16[2048,2048]{1,0:T(8,128)(2,1)}, bf16[2048,768]{1,0:T(8,128)(2,1)}, ...) custom-call(bf16[128,2048]{1,0:T(8,128)(2,1)} %bitcast.23, ...), custom_call_target="tpu_custom_call" | custom-call | tf_op jit(solution)/shard_map/pallas_call | solution.py:433
  107.5 0.8 maximum_maximum_fusion.refs_4_
  108.4 121.3 %shard_map.256 = (bf16[1024,2048]{1,0:T(8,128)(2,1)}, bf16[1024,2048]{1,0:T(8,128)(2,1)}, bf16[2048,768]{1,0:T(8,128)(2,1)}, bf16[768,2048]{1,0:T(8,128)(2,1)}, ...) custom-call(bf16[2048,768]{1,0:T(8,128)(2,1)} %get-tuple-element.59.refs_, ...), custom_call_target="tpu_custom_call" | custom-call | tf_op jit(solution)/shard_map/pallas_call | solution.py:433
  229.7 61.3 %shard_map.257 = (f32[128,2048]{1,0:T(8,128)}, f32[1,2048]{1,0:T(1,128)}, bf16[128,2048]{1,0:T(8,128)(2,1)}, bf16[1024,256]{1,0:T(8,128)(2,1)}, bf16[128,1536]{1,0:T(8,128)(2,1)}) custom-call(bf16[1024,1536]{1,0:T(8,128)(2,1)} %get-tuple-element.70.refs_0_, bf16[2048,768]{1,0:T(8,128)(2,1)} %get-tuple-element.59.refs_0_.refs_1_, ...), custom_call_target="tpu_custom_call" | custom-call | tf_op jit(solution)/shard_map/pallas_call | solution.py:433
  291.1 48.3 %shard_map.258 = (bf16[1024,768]{1,0:T(8,128)(2,1)}, f32[2,256]{1,0:T(2,128)}, bf16[128,2048]{1,0:T(8,128)(2,1)}, bf16[1024,1536]{1,0:T(8,128)(2,1)}) custom-call(bf16[1024,256]{1,0:T(8,128)(2,1)} %get-tuple-element.64.refs_0_, bf16[1024,256]{1,0:T(8,128)(2,1)} %get-tuple-element.65.refs_1_, bf16[1024,256]{1,0:T(8,128)(2,1)} %get-tuple-element.66.refs_2_, ...), custom_call_target="tpu_custom_call" | custom-call | tf_op jit(solution)/shard_map/pallas_call | solution.py:433
  340.8 3.7 convolution_convert_fusion
  344.5 2.1 pad_maximum_fusion.refs_4_
  346.6 52.1 %shard_map.259 = (f32[128,2048]{1,0:T(8,128)}, bf16[128,256]{1,0:T(8,128)(2,1)}, bf16[128,768]{1,0:T(8,128)(2,1)}, bf16[800,128]{1,0:T(8,128)(2,1)}) custom-call(bf16[1024,768]{1,0:T(8,128)(2,1)} %get-tuple-element.79.refs_0_, bf16[2048,768]{1,0:T(8,128)(2,1)} %get-tuple-element.80.refs_1_, bf16[128,2048]{1,0:T(8,128)(2,1)} %get-tuple-element.81.refs_2_, ...), custom_call_target="tpu_custom_call" | custom-call | tf_op jit(solution)/shard_map/pallas_call | solution.py:433
  398.7 1.0 broadcast_select_fusion.3
  399.7 8.4 %collective-permute-start.2 = (bf16[352,128]{1,0:T(8,128)(2,1)S(1)}, bf16[352,128]{1,0:T(8,128)(2,1)S(1)}, u32[]{:S(2)}, u32[]{:S(2)}) collective-permute-start(bf16[352,128]{1,0:T(8,128)(2,1)S(1)} %get-tuple-element.107), channel_id=1, source_target_pairs={{0,0},{1,1},{16,2},{17,3},{32,4},{33,5},{48,6},{49,7},{64,8},{65,9... | collective-permute-start | bytes 270344 | tf_op jit(solution)/shard_map/ppermute | solution.py:1393
  408.2 1.3 slice.34.refs_3_
  409.5 5.0 %shard_map.262 = (f32[128,5632]{1,0:T(8,128)}, f32[128,5632]{1,0:T(8,128)}) custom-call(bf16[1024,1536]{1,0:T(8,128)(2,1)} %get-tuple-element.100.shares), custom_call_target="tpu_custom_call" | custom-call | tf_op jit(solution)/shard_map/pallas_call | solution.py:1241
  415.2 37.6 %shard_map.260 = (bf16[1024,768]{1,0:T(8,128)(2,1)}, bf16[1024,256]{1,0:T(8,128)(2,1)}, bf16[2816,256]{1,0:T(8,128)(2,1)}, bf16[256,128]{1,0:T(8,128)(2,1)}) custom-call(bf16[128,768]{1,0:T(8,128)(2,1)} %get-tuple-element.90.refs_0_, bf16[128,256]{1,0:T(8,128)(2,1)} %get-tuple-element.91.refs_1_, bf16[352,256]{1,0:T(8,128)(2,1)} %pad_maximum_fusion.2.refs_2_, ...), custom_call_target="tpu_custom_call" | custom-call | tf_op jit(solution)/shard_map/pallas_call | solution.py:433
  452.8 0.7 convert_reduce_fusion
  454.1 7.3 %shard_map.261 = (f32[128,2048]{1,0:T(8,128)}, f32[128,2048]{1,0:T(8,128)}, f32[128,2048]{1,0:T(8,128)}, f32[128,2048]{1,0:T(8,128)}, f32[352,2048]{1,0:T(8,128)}) custom-call(bf16[1024,768]{1,0:T(8,128)(2,1)} %get-tuple-element.93.qkv, bf16[1024,256]{1,0:T(8,128)(2,1)} %get-tuple-element.94.out, bf16[2816,256]{1,0:T(8,128)(2,1)} %get-tuple-element.95.down), custom_call_target="tpu_custom_call" | custom-call | tf_op jit(solution)/shard_map/pallas_call | solution.py:1263
  461.4 0.8 copy.39
  462.2 1.0 copy.40
  (52 shorter events, 6.9 us)
Async XLA Ops:
  0.6 8.1 %copy-start = (bf16[128,5632]{1,0:T(8,128)(2,1)S(1)}, bf16[128,5632]{1,0:T(8,128)(2,1)}, u32[]{:S(2)}) copy-start(bf16[128,5632]{1,0:T(8,128)(2,1)} %param.22) | copy-start | bytes 4325380
  0.7 13.2 %copy-start.9 = (bf16[128]{0:T(256)(128)(2,1)S(1)}, bf16[128]{0:T(256)(128)(2,1)}, u32[]{:S(2)}) copy-start(bf16[128]{0:T(256)(128)(2,1)} %param.25) | copy-start | bytes 772
  0.7 13.2 %copy-start.8 = (bf16[128]{0:T(256)(128)(2,1)S(1)}, bf16[128]{0:T(256)(128)(2,1)}, u32[]{:S(2)}) copy-start(bf16[128]{0:T(256)(128)(2,1)} %param.26) | copy-start | bytes 772
  0.7 13.2 %copy-start.7 = (bf16[128]{0:T(256)(128)(2,1)S(1)}, bf16[128]{0:T(256)(128)(2,1)}, u32[]{:S(2)}) copy-start(bf16[128]{0:T(256)(128)(2,1)} %param.27) | copy-start | bytes 772
  0.7 13.1 %copy-start.6 = (bf16[128]{0:T(256)(128)(2,1)S(1)}, bf16[128]{0:T(256)(128)(2,1)}, u32[]{:S(2)}) copy-start(bf16[128]{0:T(256)(128)(2,1)} %param.28) | copy-start | bytes 772
  1.8 105.7 %collective-permute-start = (bf16[352,128]{1,0:T(8,128)(2,1)S(1)}, bf16[352,128]{1,0:T(8,128)(2,1)S(1)}, u32[]{:S(2)}, u32[]{:S(2)}) collective-permute-start(bf16[352,128]{1,0:T(8,128)(2,1)S(1)} %get-tuple-element.105), channel_id=1, source_target_pairs={{0,0},{1,1},{2,16},{3,17},{4,32},{5,33},{6,48},{7,49},{8,64},{9,65... | collective-permute-start | bytes 270344 | tf_op jit(solution)/shard_map/ppermute | solution.py:1339
  5.6 101.9 %collective-permute-start.1 = (bf16[352,128]{1,0:T(8,128)(2,1)S(1)}, bf16[352,128]{1,0:T(8,128)(2,1)S(1)}, u32[]{:S(2)}, u32[]{:S(2)}) collective-permute-start(bf16[352,128]{1,0:T(8,128)(2,1)S(1)} %get-tuple-element.106), channel_id=1, source_target_pairs={{0,1},{1,0},{2,17},{3,16},{4,33},{5,32},{6,49},{7,48},{8,65},{9,64... | collective-permute-start | bytes 270344 | tf_op jit(solution)/shard_map/ppermute | solution.py:1339
  291.0 49.7 %copy-start.5 = (f32[1,2048]{1,0:T(1,128)S(1)}, f32[1,2048]{1,0:T(1,128)}, u32[]{:S(2)}) copy-start(f32[1,2048]{1,0:T(1,128)} %get-tuple-element.86) | copy-start | bytes 24580
  291.0 49.7 %copy-start.4 = (f32[1,2048]{1,0:T(1,128)S(1)}, f32[1,2048]{1,0:T(1,128)}, u32[]{:S(2)}) copy-start(f32[1,2048]{1,0:T(1,128)} %get-tuple-element.87) | copy-start | bytes 24580
  291.0 49.7 %copy-start.10 = (bf16[1024,2048]{1,0:T(8,128)(2,1)S(1)}, bf16[1024,2048]{1,0:T(8,128)(2,1)}, u32[]{:S(2)}) copy-start(bf16[1024,2048]{1,0:T(8,128)(2,1)} %get-tuple-element.84) | copy-start | bytes 12582916
  291.0 49.7 %copy-start.11 = (bf16[1024,768]{1,0:T(8,128)(2,1)S(1)}, bf16[1024,768]{1,0:T(8,128)(2,1)}, u32[]{:S(2)}) copy-start(bf16[1024,768]{1,0:T(8,128)(2,1)} %get-tuple-element.83) | copy-start | bytes 4718596
  399.7 14.8 %collective-permute-start.2 = (bf16[352,128]{1,0:T(8,128)(2,1)S(1)}, bf16[352,128]{1,0:T(8,128)(2,1)S(1)}, u32[]{:S(2)}, u32[]{:S(2)}) collective-permute-start(bf16[352,128]{1,0:T(8,128)(2,1)S(1)} %get-tuple-element.107), channel_id=1, source_target_pairs={{0,0},{1,1},{16,2},{17,3},{32,4},{33,5},{48,6},{49,7},{64,8},{65,9... | collective-permute-start | bytes 270344 | tf_op jit(solution)/shard_map/ppermute | solution.py:1393
  408.1 6.4 %collective-permute-start.3 = (bf16[352,128]{1,0:T(8,128)(2,1)S(1)}, bf16[352,128]{1,0:T(8,128)(2,1)S(1)}, u32[]{:S(2)}, u32[]{:S(2)}) collective-permute-start(bf16[352,128]{1,0:T(8,128)(2,1)S(1)} %get-tuple-element.108), channel_id=1, source_target_pairs={{1,0},{0,1},{17,2},{16,3},{33,4},{32,5},{49,6},{48,7},{65,8},{64,9... | collective-permute-start | bytes 270344 | tf_op jit(solution)/shard_map/ppermute | solution.py:1393
  414.5 47.0 %copy-start.3 = (bf16[128,2048]{1,0:T(8,128)(2,1)S(1)}, bf16[128,2048]{1,0:T(8,128)(2,1)}, u32[]{:S(2)}) copy-start(bf16[128,2048]{1,0:T(8,128)(2,1)} %get-tuple-element.63) | copy-start | bytes 1572868
  414.5 47.8 %copy-start.2 = (f32[128,2048]{1,0:T(8,128)S(1)}, f32[128,2048]{1,0:T(8,128)}, u32[]{:S(2)}) copy-start(f32[128,2048]{1,0:T(8,128)} %get-tuple-element.89) | copy-start | bytes 3145732
  454.1 9.1 %copy-start.1 = (bf16[128,5632]{1,0:T(8,128)(2,1)S(1)}, bf16[128,5632]{1,0:T(8,128)(2,1)}, u32[]{:S(2)}) copy-start(bf16[128,5632]{1,0:T(8,128)(2,1)} %param.22) | copy-start | bytes 4325380

commit v3 on v2

--- a/solution.py
+++ b/solution.py
@@ -1250,10 +1250,14 @@
 
 def widen_kernel(qkv, out, down, query_out, key_out, value_out, out_out, down_out):
     share = out.shape[1]
-    for i, ref in enumerate((query_out, key_out, value_out)):
-        ref[...] = qkv[:, pl.ds(i * share, share)].astype(F32)
-    out_out[...] = out[...].astype(F32)
-    down_out[...] = down[...].astype(F32)
+    for half in range(2):
+        at = pl.ds(half * share, share)
+        rows = pl.ds(half * query_out.shape[0], query_out.shape[0])
+        for i, ref in enumerate((query_out, key_out, value_out)):
+            ref[:, at] = qkv[rows, pl.ds(i * share, share)].astype(F32)
+        out_out[:, at] = out[rows, :].astype(F32)
+        size = down_out.shape[0]
+        down_out[:, at] = down[pl.ds(half * size, size), :].astype(F32)
 
 
 def widen(qkv, out, down):
@@ -1262,12 +1266,12 @@
     heights = [part.shape[0] // ranks for part in (qkv, qkv, qkv, out, down)]
     return pl.pallas_call(
         widen_kernel,
-        grid=(ranks,),
+        grid=(ranks // 2,),
         in_specs=[
-            pl.BlockSpec((part.shape[0] // ranks, part.shape[1]), lambda i: (i, 0))
+            pl.BlockSpec((part.shape[0] // ranks * 2, part.shape[1]), lambda i: (i, 0))
             for part in (qkv, out, down)
         ],
-        out_specs=[pl.BlockSpec((height, share), lambda i: (0, i)) for height in heights],
+        out_specs=[pl.BlockSpec((height, 2 * share), lambda i: (0, i)) for height in heights],
         out_shape=[shape((height, ranks * share), F32) for height in heights],
         compiler_params=pltpu.CompilerParams(vmem_limit_bytes=ROOM),
     )(qkv, out, down)
@@ -1373,21 +1377,25 @@
     outer = attend_back(
         front, inner.mixed_grad, cosine, sine, orders, inner.gate_up_share, inner.attn_low, 4
     )
-    down_grad = low(outer_sum(fed.product, fed.whole_down))
 
     def placed(term):
         return lax.dynamic_update_slice_in_dim(
             jnp.zeros((width,), F32), term, rank * share, axis=0
         )
 
-    gain_terms = low(jnp.stack([placed(outer.terms[0]), placed(outer.terms[1]), inner.attn_term[0], fed.feed_term[0]]))
-    strip_grads = jnp.concatenate([down_grad, jnp.pad(gain_terms, ((0, 28), (0, 0)))], axis=0)
+    gain_terms = jnp.stack(
+        [placed(outer.terms[0]), placed(outer.terms[1]), inner.attn_term[0], fed.feed_term[0]]
+    )
+    strip_grads = low(
+        outer_sum(fed.product, fed.whole_down)
+        + jnp.pad(gain_terms, ((units, room - units - gain_terms.shape[0]), (0, 0)))
+    )
     last = input_back(
         outer.qkv_low, front.qkv, inner.hidden_grad, outer.out_share, front.whole, strip_grads, 5
     )
     down_size = down_weight.shape[0]
     by_owner = [last.strip_share[j * down_size : (j + 1) * down_size] for j in range(2)]
-    gains_share = last.strip_share[room:]
+    gains_share = last.strip_share[units : units + 32]
     by_route = in_order(by_owner)
     returned = [
         lax.ppermute(piece, axes, [(b, a) for a, b in route])

time: 471 us -> 466 us (0.989)
  no operation moved by 1% of the time
where the time goes in v3:
time: 466 us; the launch traced here: 460 us
  Pallas kernels  424 us (91%)
  starting transfers between devices  12.7 us (3%)
  local copies, waits for them, and re-layouts  12.5 us (3%)
  other arithmetic  5.32 us (1%)
  matrix products  4.88 us (1%)
    pallas_call x6, Pallas kernels, launch(): pl.pallas_call(kernel, out_shape=[out for out, _ in outs.values()], in_sp...  413 us
  transfers between devices with their start and end apart: 4, of which 0 were waited for; matrix products, arithmetic and copies ran while one was open for 2% of the time, Pallas kernels for 21%

profile of v3, /device:TPU:2, one launch (start us, length us, event | category | flops | bytes accessed | tf_op | source)
XLA Modules:
  0.0 460.3 jit_solution(2584726106087973989)
XLA Ops:
  0.7 1.1 constant_dynamic-slice_fusion.1
  1.8 3.8 collective-permute-start
  6.8 1.3 add.79.refs_7_.refs_13_
  8.9 1.1 constant_dynamic-slice_fusion.2
  9.9 0.7 pad.16.refs_4_
  10.6 0.7 pad.17.refs_3_
  11.4 0.8 constant_dynamic-slice_fusion.6
  12.2 0.9 constant_dynamic-slice_fusion.4
  14.4 93.0 %shard_map.255 = (bf16[1024,2048]{1,0:T(8,128)(2,1)}, bf16[2048,768]{1,0:T(8,128)(2,1)}, bf16[2048,2048]{1,0:T(8,128)(2,1)}, bf16[2048,768]{1,0:T(8,128)(2,1)}, ...) custom-call(bf16[128,2048]{1,0:T(8,128)(2,1)} %bitcast.23, ...), custom_call_target="tpu_custom_call" | custom-call | tf_op jit(solution)/shard_map/pallas_call | solution.py:433
  107.5 0.8 maximum_maximum_fusion.refs_4_
  108.4 121.3 %shard_map.256 = (bf16[1024,2048]{1,0:T(8,128)(2,1)}, bf16[1024,2048]{1,0:T(8,128)(2,1)}, bf16[2048,768]{1,0:T(8,128)(2,1)}, bf16[768,2048]{1,0:T(8,128)(2,1)}, ...) custom-call(bf16[2048,768]{1,0:T(8,128)(2,1)} %get-tuple-element.59.refs_, ...), custom_call_target="tpu_custom_call" | custom-call | tf_op jit(solution)/shard_map/pallas_call | solution.py:433
  229.6 61.3 %shard_map.257 = (f32[128,2048]{1,0:T(8,128)}, f32[1,2048]{1,0:T(1,128)}, bf16[128,2048]{1,0:T(8,128)(2,1)}, bf16[1024,256]{1,0:T(8,128)(2,1)}, bf16[128,1536]{1,0:T(8,128)(2,1)}) custom-call(bf16[1024,1536]{1,0:T(8,128)(2,1)} %get-tuple-element.70.refs_0_, bf16[2048,768]{1,0:T(8,128)(2,1)} %get-tuple-element.59.refs_0_.refs_1_, ...), custom_call_target="tpu_custom_call" | custom-call | tf_op jit(solution)/shard_map/pallas_call | solution.py:433
  290.9 48.1 %shard_map.258 = (bf16[1024,768]{1,0:T(8,128)(2,1)}, f32[2,256]{1,0:T(2,128)}, bf16[128,2048]{1,0:T(8,128)(2,1)}, bf16[1024,1536]{1,0:T(8,128)(2,1)}) custom-call(bf16[1024,256]{1,0:T(8,128)(2,1)} %get-tuple-element.64.refs_0_, bf16[1024,256]{1,0:T(8,128)(2,1)} %get-tuple-element.65.refs_1_, bf16[1024,256]{1,0:T(8,128)(2,1)} %get-tuple-element.66.refs_2_, ...), custom_call_target="tpu_custom_call" | custom-call | tf_op jit(solution)/shard_map/pallas_call | solution.py:433
  340.4 4.9 %fusion.1.refs_4_ = bf16[768,2048]{1,0:T(8,128)(2,1)} fusion(f32[1,2048]{1,0:T(1,128)S(1)} %copy-done.10, f32[1,2048]{1,0:T(1,128)S(1)} %copy-done.11, f32[1,2048]{1,0:T(1,128)S(1)} %constant_dynamic-update-slice_fusion, f32[1,2048]{1,0:T(1,128)S(1)} %constant_dynamic-update-slice_fusion.1, bf16[1024,768]{1,0:T(8,128)(2,1)S(1)} %copy-done.9, ...), kind=kOutput, calls=%fused_computation.4 | convolution fusion | flops 3240099840 | bytes 8945664 | tf_op jit(solution)/shard_map/dot_general | solution.py:33
  345.3 51.5 %shard_map.259 = (f32[128,2048]{1,0:T(8,128)}, bf16[128,256]{1,0:T(8,128)(2,1)}, bf16[128,768]{1,0:T(8,128)(2,1)}, bf16[768,128]{1,0:T(8,128)(2,1)}) custom-call(bf16[1024,768]{1,0:T(8,128)(2,1)} %get-tuple-element.79.refs_0_, bf16[2048,768]{1,0:T(8,128)(2,1)} %get-tuple-element.80.refs_1_, bf16[128,2048]{1,0:T(8,128)(2,1)} %get-tuple-element.81.refs_2_, ...), custom_call_target="tpu_custom_call" | custom-call | tf_op jit(solution)/shard_map/pallas_call | solution.py:433
  396.8 1.0 broadcast_select_fusion.3
  397.7 8.6 %collective-permute-start.2 = (bf16[352,128]{1,0:T(8,128)(2,1)S(1)}, bf16[352,128]{1,0:T(8,128)(2,1)S(1)}, u32[]{:S(2)}, u32[]{:S(2)}) collective-permute-start(bf16[352,128]{1,0:T(8,128)(2,1)S(1)} %get-tuple-element.107), channel_id=1, source_target_pairs={{0,0},{1,1},{16,2},{17,3},{32,4},{33,5},{48,6},{49,7},{64,8},{65,9... | collective-permute-start | bytes 270344 | tf_op jit(solution)/shard_map/ppermute | solution.py:1401
  406.4 1.3 slice.34.refs_3_
  407.7 5.0 %shard_map.262 = (f32[128,5632]{1,0:T(8,128)}, f32[128,5632]{1,0:T(8,128)}) custom-call(bf16[1024,1536]{1,0:T(8,128)(2,1)} %get-tuple-element.100.shares), custom_call_target="tpu_custom_call" | custom-call | tf_op jit(solution)/shard_map/pallas_call | solution.py:1241
  413.4 38.2 %shard_map.260 = (bf16[1024,768]{1,0:T(8,128)(2,1)}, bf16[1024,256]{1,0:T(8,128)(2,1)}, bf16[2816,256]{1,0:T(8,128)(2,1)}, bf16[256,128]{1,0:T(8,128)(2,1)}) custom-call(bf16[128,768]{1,0:T(8,128)(2,1)} %get-tuple-element.90.refs_0_, bf16[128,256]{1,0:T(8,128)(2,1)} %get-tuple-element.91.refs_1_, bf16[352,256]{1,0:T(8,128)(2,1)} %pad_maximum_fusion.1.refs_2_, ...), custom_call_target="tpu_custom_call" | custom-call | tf_op jit(solution)/shard_map/pallas_call | solution.py:433
  451.6 0.7 convert_reduce_fusion
  452.9 5.4 %shard_map.261 = (f32[128,2048]{1,0:T(8,128)}, f32[128,2048]{1,0:T(8,128)}, f32[128,2048]{1,0:T(8,128)}, f32[128,2048]{1,0:T(8,128)}, f32[352,2048]{1,0:T(8,128)}) custom-call(bf16[1024,768]{1,0:T(8,128)(2,1)} %get-tuple-element.93.qkv, bf16[1024,256]{1,0:T(8,128)(2,1)} %get-tuple-element.94.out, bf16[2816,256]{1,0:T(8,128)(2,1)} %get-tuple-element.95.down), custom_call_target="tpu_custom_call" | custom-call | tf_op jit(solution)/shard_map/pallas_call | solution.py:1267
  458.2 0.8 copy.37
  459.0 1.0 copy.38
  (48 shorter events, 6.1 us)
Async XLA Ops:
  0.6 8.1 %copy-start = (bf16[128,5632]{1,0:T(8,128)(2,1)S(1)}, bf16[128,5632]{1,0:T(8,128)(2,1)}, u32[]{:S(2)}) copy-start(bf16[128,5632]{1,0:T(8,128)(2,1)} %param.22) | copy-start | bytes 4325380
  0.7 13.2 %copy-start.7 = (bf16[128]{0:T(256)(128)(2,1)S(1)}, bf16[128]{0:T(256)(128)(2,1)}, u32[]{:S(2)}) copy-start(bf16[128]{0:T(256)(128)(2,1)} %param.25) | copy-start | bytes 772
  0.7 13.2 %copy-start.6 = (bf16[128]{0:T(256)(128)(2,1)S(1)}, bf16[128]{0:T(256)(128)(2,1)}, u32[]{:S(2)}) copy-start(bf16[128]{0:T(256)(128)(2,1)} %param.26) | copy-start | bytes 772
  0.7 13.2 %copy-start.5 = (bf16[128]{0:T(256)(128)(2,1)S(1)}, bf16[128]{0:T(256)(128)(2,1)}, u32[]{:S(2)}) copy-start(bf16[128]{0:T(256)(128)(2,1)} %param.27) | copy-start | bytes 772
  0.7 13.1 %copy-start.4 = (bf16[128]{0:T(256)(128)(2,1)S(1)}, bf16[128]{0:T(256)(128)(2,1)}, u32[]{:S(2)}) copy-start(bf16[128]{0:T(256)(128)(2,1)} %param.28) | copy-start | bytes 772
  1.8 105.7 %collective-permute-start = (bf16[352,128]{1,0:T(8,128)(2,1)S(1)}, bf16[352,128]{1,0:T(8,128)(2,1)S(1)}, u32[]{:S(2)}, u32[]{:S(2)}) collective-permute-start(bf16[352,128]{1,0:T(8,128)(2,1)S(1)} %get-tuple-element.105), channel_id=1, source_target_pairs={{0,0},{1,1},{2,16},{3,17},{4,32},{5,33},{6,48},{7,49},{8,64},{9,65... | collective-permute-start | bytes 270344 | tf_op jit(solution)/shard_map/ppermute | solution.py:1343
  5.6 101.9 %collective-permute-start.1 = (bf16[352,128]{1,0:T(8,128)(2,1)S(1)}, bf16[352,128]{1,0:T(8,128)(2,1)S(1)}, u32[]{:S(2)}, u32[]{:S(2)}) collective-permute-start(bf16[352,128]{1,0:T(8,128)(2,1)S(1)} %get-tuple-element.106), channel_id=1, source_target_pairs={{0,1},{1,0},{2,17},{3,16},{4,33},{5,32},{6,49},{7,48},{8,65},{9,64... | collective-permute-start | bytes 270344 | tf_op jit(solution)/shard_map/ppermute | solution.py:1343
  290.9 49.5 %copy-start.8 = (bf16[1024,2048]{1,0:T(8,128)(2,1)S(1)}, bf16[1024,2048]{1,0:T(8,128)(2,1)}, u32[]{:S(2)}) copy-start(bf16[1024,2048]{1,0:T(8,128)(2,1)} %get-tuple-element.84) | copy-start | bytes 12582916
  290.9 49.5 %copy-start.9 = (bf16[1024,768]{1,0:T(8,128)(2,1)S(1)}, bf16[1024,768]{1,0:T(8,128)(2,1)}, u32[]{:S(2)}) copy-start(bf16[1024,768]{1,0:T(8,128)(2,1)} %get-tuple-element.83) | copy-start | bytes 4718596
  290.9 49.4 %copy-start.10 = (f32[1,2048]{1,0:T(1,128)S(1)}, f32[1,2048]{1,0:T(1,128)}, u32[]{:S(2)}) copy-start(f32[1,2048]{1,0:T(1,128)} %get-tuple-element.87) | copy-start | bytes 24580
  290.9 49.4 %copy-start.11 = (f32[1,2048]{1,0:T(1,128)S(1)}, f32[1,2048]{1,0:T(1,128)}, u32[]{:S(2)}) copy-start(f32[1,2048]{1,0:T(1,128)} %get-tuple-element.86) | copy-start | bytes 24580
  397.7 15.0 %collective-permute-start.2 = (bf16[352,128]{1,0:T(8,128)(2,1)S(1)}, bf16[352,128]{1,0:T(8,128)(2,1)S(1)}, u32[]{:S(2)}, u32[]{:S(2)}) collective-permute-start(bf16[352,128]{1,0:T(8,128)(2,1)S(1)} %get-tuple-element.107), channel_id=1, source_target_pairs={{0,0},{1,1},{16,2},{17,3},{32,4},{33,5},{48,6},{49,7},{64,8},{65,9... | collective-permute-start | bytes 270344 | tf_op jit(solution)/shard_map/ppermute | solution.py:1401
  406.3 6.4 %collective-permute-start.3 = (bf16[352,128]{1,0:T(8,128)(2,1)S(1)}, bf16[352,128]{1,0:T(8,128)(2,1)S(1)}, u32[]{:S(2)}, u32[]{:S(2)}) collective-permute-start(bf16[352,128]{1,0:T(8,128)(2,1)S(1)} %get-tuple-element.108), channel_id=1, source_target_pairs={{1,0},{0,1},{17,2},{16,3},{33,4},{32,5},{49,6},{48,7},{65,8},{64,9... | collective-permute-start | bytes 270344 | tf_op jit(solution)/shard_map/ppermute | solution.py:1401
  412.7 45.6 %copy-start.3 = (bf16[128,2048]{1,0:T(8,128)(2,1)S(1)}, bf16[128,2048]{1,0:T(8,128)(2,1)}, u32[]{:S(2)}) copy-start(bf16[128,2048]{1,0:T(8,128)(2,1)} %get-tuple-element.63) | copy-start | bytes 1572868
  412.7 46.3 %copy-start.2 = (f32[128,2048]{1,0:T(8,128)S(1)}, f32[128,2048]{1,0:T(8,128)}, u32[]{:S(2)}) copy-start(f32[128,2048]{1,0:T(8,128)} %get-tuple-element.89) | copy-start | bytes 3145732
  452.9 7.2 %copy-start.1 = (bf16[128,5632]{1,0:T(8,128)(2,1)S(1)}, bf16[128,5632]{1,0:T(8,128)(2,1)}, u32[]{:S(2)}) copy-start(bf16[128,5632]{1,0:T(8,128)(2,1)} %param.22) | copy-start | bytes 4325380
